TPU v7x, 512 devices: a whole 4x4x16 slice. The times are simulated.
512 devices in a mesh: member: 16 (over y, z_hi, core), gx: 32 (over x, z_lo).
Axes of the slice: x: 4, y: 4, z: 16 (z_hi: 2, z_lo: 8; z = z_hi * 8 + z_lo), core: 2. Of those that a mesh axis runs over, the one named last changes fastest.
Arguments:
- features: bfloat16 [16, 64, 8, 32, 128], P('member', 'gx'), may hold values from -6 to 6
- cotangent: bfloat16 [16, 64, 8, 32, 128], P('member', 'gx'), may hold values from -6 to 6
- keep_flags: int32 [16, 3], P('member'), may hold values from 0 to 1, as said below
- conv_a: bfloat16 [27, 128, 128], replicated, may hold values from -0.109375 to 0.109375
- conv_b: bfloat16 [27, 128, 128], replicated, may hold values from -0.109375 to 0.109375
- conv_c: bfloat16 [27, 512, 512], P(None, None, 'gx'), may hold values from -0.1875 to 0.1875
- lift_one: bfloat16 [128, 128], replicated, may hold values from -0.5 to 0.5
- lift_two: bfloat16 [128, 512], replicated, may hold values from -0.5 to 0.5
- lower_two: bfloat16 [512, 128], replicated, may hold values from -0.25 to 0.25
- lower_one: bfloat16 [128, 128], replicated, may hold values from -0.5 to 0.5
Outputs:
- result: bfloat16 [16, 64, 8, 32, 128], P('member', 'gx')
- grad_conv_a: float32 [27, 128, 128], P(None, None, 'gx')
- grad_conv_b: float32 [27, 128, 128], P(None, None, 'gx')
- grad_conv_c: float32 [27, 512, 512], P(None, None, 'gx')
Inputs may be any that keep to these rules, and one draw needn't show every extreme that they name: `keep_flags`: 1 where the member keeps the block, 0 where it is dropped; every block is kept by at least one member.
All inputs are finite; a program needn't handle non-finite values.
Results may differ from a plain program's by a relative error of at most 0.024.
Values may be sent and summed in bfloat16 or wider, within the bound.
A program may use at most 64 MiB of HBM per device.

v0:
```python
import jax
import jax.numpy as jnp
from jax import lax
from jax.sharding import PartitionSpec as P

survival = (0.9, 0.8, 0.7)


def extended(x, sides, width):
    for axis, dim in sides:
        size, length = (lax.axis_size(axis), x.shape[dim])
        up = [(i, (i + 1) % size) for i in range(size - 1)]
        down = [(j, i) for i, j in up]
        last = lax.slice_in_dim(x, length - width, length, axis=dim)
        first = lax.slice_in_dim(x, 0, width, axis=dim)
        before = lax.ppermute(last, axis, up)
        after = lax.ppermute(first, axis, down)
        x = jnp.concatenate([before, x, after], axis=dim)
    return x


def offsets(position):
    return (position // 9 - 1, position // 3 % 3 - 1, position % 3 - 1)


def padded3(field_in):
    return jnp.pad(field_in, ((1, 1), (1, 1), (1, 1), (0, 0)))


def window(padded, grid_shape, shift_x, shift_y, shift_z):
    return padded[
        1 + shift_x : 1 + shift_x + grid_shape[0],
        1 + shift_y : 1 + shift_y + grid_shape[1],
        1 + shift_z : 1 + shift_z + grid_shape[2],
        :,
    ]


def flatten(field_in):
    return field_in.reshape(-1, field_in.shape[-1])


def project(field_in, matrix):
    return jnp.dot(flatten(field_in), matrix, preferred_element_type=jnp.float32).reshape(
        field_in.shape[:-1] + (matrix.shape[1],)
    )


def slope(value):
    logistic = jax.nn.sigmoid(value)
    return logistic * (1.0 + value * (1.0 - logistic))


def mean_yz(field_in):
    sizes_now = field_in.shape
    return field_in.reshape(
        sizes_now[0], sizes_now[1] // 2, 2, sizes_now[2] // 2, 2, sizes_now[3]
    ).mean(axis=(2, 4))


def sum_yz(field_in):
    sizes_now = field_in.shape
    return (
        field_in.astype(jnp.float32)
        .reshape(sizes_now[0], sizes_now[1] // 2, 2, sizes_now[2] // 2, 2, sizes_now[3])
        .sum(axis=(2, 4))
    )


def mean_pairs(field_in):
    sizes_now = field_in.shape
    return field_in.reshape((sizes_now[0] // 2, 2) + sizes_now[1:]).mean(axis=1)


def sum_pairs(field_in):
    sizes_now = field_in.shape
    return field_in.reshape((sizes_now[0] // 2, 2) + sizes_now[1:]).sum(axis=1)


def mean_cubes(field_in):
    sizes_now = field_in.shape
    return field_in.reshape(
        sizes_now[0] // 2, 2, sizes_now[1] // 2, 2, sizes_now[2] // 2, 2, sizes_now[3]
    ).mean(axis=(1, 3, 5))


def sum_cubes(field_in):
    sizes_now = field_in.shape
    return (
        field_in.astype(jnp.float32)
        .reshape(sizes_now[0] // 2, 2, sizes_now[1] // 2, 2, sizes_now[2] // 2, 2, sizes_now[3])
        .sum(axis=(1, 3, 5))
    )


def grow_cubes(field_in):
    return jnp.repeat(jnp.repeat(jnp.repeat(field_in, 2, axis=0), 2, axis=1), 2, axis=2)


def grow_yz(field_in):
    return jnp.repeat(jnp.repeat(field_in, 2, axis=1), 2, axis=2)


def yz_stack(padded_x):
    grid_y = padded_x.shape[1]
    grid_z = padded_x.shape[2]
    padded = jnp.pad(padded_x, ((0, 0), (1, 1), (1, 1), (0, 0)))
    pieces = []
    for shift_y in (-1, 0, 1):
        for shift_z in (-1, 0, 1):
            pieces.append(
                padded[:, 1 + shift_y : 1 + shift_y + grid_y, 1 + shift_z : 1 + shift_z + grid_z, :]
            )
    return jnp.concatenate(pieces, axis=3)


def slab_conv(stack, weight, planes):
    width_in, width_out = (weight.shape[1], weight.shape[2])
    running = jnp.zeros((planes,) + stack.shape[1:3] + (width_out,), jnp.float32)
    for shift_x in (-1, 0, 1):
        first_tap = (shift_x + 1) * 9
        window_piece = stack[1 + shift_x : 1 + shift_x + planes]
        running = running + project(
            window_piece, weight[first_tap : first_tap + 9].reshape(9 * width_in, width_out)
        )
    return running


def slab_wgrad(stack, gradient):
    planes = gradient.shape[0]
    width_in = stack.shape[3] // 9
    results = []
    for shift_x in (-1, 0, 1):
        window_piece = stack[1 + shift_x : 1 + shift_x + planes]
        product = jnp.dot(
            flatten(window_piece).T, flatten(gradient), preferred_element_type=jnp.float32
        )
        results.append(product.reshape(9, width_in, gradient.shape[-1]))
    return jnp.concatenate(results, axis=0)


def back_stack(padded, grid_shape):
    pieces = []
    for position in range(27):
        shift_x, shift_y, shift_z = offsets(position)
        pieces.append(window(padded, grid_shape, -shift_x, -shift_y, -shift_z))
    return jnp.concatenate(pieces, axis=3)


def stacked_conv(hidden, weight):
    width_in, width_out = (weight.shape[1], weight.shape[2])
    weight_table = weight.transpose(1, 0, 2).reshape(width_in, 27 * width_out)
    padded = padded3(project(hidden, weight_table))
    running = jnp.zeros(hidden.shape[:3] + (width_out,), jnp.float32)
    for position in range(27):
        shift_x, shift_y, shift_z = offsets(position)
        window_piece = window(padded, hidden.shape, shift_x, shift_y, shift_z)
        running = running + window_piece[..., position * width_out : (position + 1) * width_out]
    return running


def stacked_back(stack, weight):
    width_in, width_out = (weight.shape[1], weight.shape[2])
    return project(stack, weight.transpose(0, 2, 1).reshape(27 * width_out, width_in))


def stacked_wgrad(hidden, stack, width_out):
    width_in = hidden.shape[-1]
    product = jnp.dot(flatten(hidden).T, flatten(stack), preferred_element_type=jnp.float32)
    return product.reshape(width_in, 27, width_out).transpose(1, 0, 2)


def body(
    features,
    cotangent,
    keep_flags,
    conv_a,
    conv_b,
    conv_c,
    lift_one,
    lift_two,
    lower_two,
    lower_one,
):
    bf16 = jnp.bfloat16
    f32 = jnp.float32
    device = lax.axis_index("gx")
    width_c = conv_c.shape[2]
    start_c = device * width_c
    plane_index = device // 2
    scales = keep_flags[0].astype(f32) / jnp.array(survival, f32)
    own_plane = features[0]
    planes = own_plane.shape[0]
    hidden_a = jax.nn.silu(own_plane.astype(f32)).astype(bf16)
    padded_a = extended(hidden_a, (("gx", 0),), 1)
    stack_a = yz_stack(padded_a)
    level_a = own_plane.astype(f32) + scales[0] * slab_conv(stack_a, conv_a, planes)
    pooled_one = mean_cubes(level_a).astype(bf16)
    level_in_b = project(pooled_one, lift_one).astype(bf16)
    hidden_b = jax.nn.silu(level_in_b.astype(f32)).astype(bf16)
    padded_b = extended(hidden_b, (("gx", 0),), 1)
    stack_b = yz_stack(padded_b)
    level_b = level_in_b.astype(f32) + scales[1] * slab_conv(stack_b, conv_b, level_in_b.shape[0])
    halves_b = mean_yz(level_b)
    planes_b = lax.all_gather(halves_b, "gx", axis=0, tiled=True)
    pooled_two = mean_pairs(planes_b).astype(bf16)
    level_in_c = project(pooled_two, lift_two).astype(bf16)
    hidden_c = jax.nn.silu(level_in_c.astype(f32)).astype(bf16)
    input_shard_c = lax.dynamic_slice_in_dim(level_in_c, start_c, width_c, 3)
    level_c = (input_shard_c.astype(f32) + scales[2] * stacked_conv(hidden_c, conv_c)).astype(bf16)
    lower_rows = lax.dynamic_slice_in_dim(lower_two, start_c, width_c, 0)
    expanded_all = lax.psum(project(level_c, lower_rows), "gx")
    expanded = lax.dynamic_slice_in_dim(expanded_all, plane_index, 1, 0)
    level_d = (level_b + grow_yz(expanded)).astype(bf16)
    result = (level_a + grow_cubes(project(level_d, lower_one))).astype(bf16)
    upstream = cotangent[0]
    grad_e1 = sum_cubes(upstream).astype(bf16)
    grad_d = project(grad_e1, lower_one.T).astype(bf16)
    grad_halves = sum_yz(grad_d)
    grad_planes = lax.all_gather(grad_halves, "gx", axis=0, tiled=True)
    grad_e2 = sum_pairs(grad_planes).astype(bf16)
    grad_c = project(grad_e2, lower_two.T).astype(bf16)
    grad_c_shard = lax.dynamic_slice_in_dim(grad_c, start_c, width_c, 3)
    stack_c = back_stack(padded3(grad_c_shard), grad_c_shard.shape)
    weight_c_term = scales[2] * stacked_wgrad(hidden_c, stack_c, width_c)
    back_c = lax.psum(stacked_back(stack_c, conv_c), "gx")
    back_plane = lax.dynamic_slice_in_dim(back_c, plane_index, 1, 0)
    grad_c_plane = lax.dynamic_slice_in_dim(grad_c, plane_index, 1, 0)
    level_in_plane = lax.dynamic_slice_in_dim(level_in_c, plane_index, 1, 0)
    grad_q = (
        grad_c_plane.astype(f32) + scales[2] * slope(level_in_plane.astype(f32)) * back_plane
    ).astype(bf16)
    grad_m2 = project(grad_q, lift_two.T).astype(bf16)
    grad_b = (grad_d.astype(f32) + grow_yz(grad_m2.astype(f32)) / 8.0).astype(bf16)
    padded_grad_b = extended(grad_b, (("gx", 0),), 1)
    padded_grad_b = jnp.pad(padded_grad_b, ((0, 0), (1, 1), (1, 1), (0, 0)))
    stack_grad_b = back_stack(padded_grad_b, grad_b.shape)
    weight_b_term = scales[1] * stacked_wgrad(hidden_b, stack_grad_b, conv_b.shape[2])
    back_b = stacked_back(stack_grad_b, conv_b)
    weight_b_part = lax.psum_scatter(weight_b_term, "gx", scatter_dimension=2, tiled=True)
    grad_p = (grad_b.astype(f32) + scales[1] * slope(level_in_b.astype(f32)) * back_b).astype(bf16)
    grad_m1 = project(grad_p, lift_one.T).astype(bf16)
    grad_a = (upstream.astype(f32) + grow_cubes(grad_m1.astype(f32)) / 8.0).astype(bf16)
    weight_a_term = scales[0] * slab_wgrad(stack_a, grad_a)
    weight_a_part = lax.psum_scatter(weight_a_term, "gx", scatter_dimension=2, tiled=True)
    weight_a_part, weight_b_part, weight_c_term = lax.psum(
        (weight_a_part, weight_b_part, weight_c_term), "member"
    )
    return (result[None], weight_a_part, weight_b_part, weight_c_term)


def solution(mesh):
    return jax.shard_map(
        body,
        mesh=mesh,
        in_specs=(
            P("member", "gx", None, None, None),
            P("member", "gx", None, None, None),
            P("member", None),
            P(),
            P(),
            P(None, None, "gx"),
            P(),
            P(),
            P(),
            P(),
        ),
        out_specs=(
            P("member", "gx", None, None, None),
            P(None, None, "gx"),
            P(None, None, "gx"),
            P(None, None, "gx"),
        ),
        check_vma=False,
    )
```

profile of v0, /device:TPU:1, one launch (start us, length us, event | category | flops | bytes accessed | tf_op | source)
XLA Modules:
  0.0 1505.5 jit_solution(15261718137668869576)
XLA Ops:
  8.1 1.1 fusion.25
  9.8 1.3 collective-permute-start.1
  11.1 5.6 collective-permute-start
  16.7 0.9 convert_reduce_fusion
  17.8 0.9 fusion.9
  18.7 110.2 %all-gather.1 = f32[64,8,128]{2,1,0:T(8,128)S(1)} all-gather(f32[2,8,128]{2,1,0:T(8,128)S(1)} %reduce_sum.78), channel_id=3, replica_groups=mesh['member'=16,'gx'=32] {'gx'}, dimensions={0}, use_global_device_ids=true | all-gather | bytes 270336 | tf_op jit(solution)/shard_map/all_gather | solution.py:220
  128.9 1.1 convolution_convert_fusion
  130.2 0.8 pad_slice_fusion.27
  131.1 0.9 fusion.114
  132.0 1.6 concatenate.85
  133.6 1.1 fusion.121
  134.7 0.7 fusion.118
  135.4 0.9 pad_maximum_fusion
  136.7 0.9 constant_dynamic-update-slice_fusion
  139.1 1.8 fusion.119
  141.1 1.3 collective-permute-start.3
  142.4 4.0 collective-permute-start.2
  146.4 1.2 fusion.113
  148.3 0.9 fusion.5
  149.3 100.8 %all-gather = f32[64,8,128]{2,1,0:T(8,128)S(1)} all-gather(f32[2,8,128]{2,1,0:T(8,128)S(1)} %broadcast_multiply_fusion), channel_id=2, replica_groups=mesh['member'=16,'gx'=32] {'gx'}, dimensions={0}, use_global_device_ids=true | all-gather | bytes 270336 | tf_op jit(solution)/shard_map/all_gather | solution.py:205
  250.0 0.7 reduce_sum.74
  250.7 1.3 fusion.16
  252.7 2.7 fusion.74
  255.5 2.2 copy.58
  257.7 448.7 %all-reduce.13.cloned.1.call-done = (f32[16,2,8,128]{3,2,1,0:T(8,128)}, f32[16,2,8,512]{3,2,1,0:T(8,128)}) async-done(((f32[16,2,8,128]{3,2,1,0:T(8,128)}, f32[16,2,8,512]{3,2,1,0:T(8,128)}), (f32[16,2,8,128]{3,2,1,0:T(8,128)}, f32[16,2,8,512]{3,2,1,0:T(8,128)})) %all-reduce.13.cloned.1.call-update) | async-done | bytes 655376 | tf_op jit(solution)/shard_map/psum | solution.py:212
  706.4 1.7 fusion.12
  708.1 1.3 collective-permute-start.5
  709.4 4.3 collective-permute-start.4
  713.7 1.9 fusion.112
  715.6 2.6 copy.60
  718.1 1.5 copy.59
  719.6 1.4 copy.56
  721.1 0.7 fusion.116
  722.9 0.8 copy-done.12
  723.7 2.4 fusion.8
  727.8 0.7 maximum_multiply_fusion
  728.7 2.3 copy.61
  731.7 1.1 multiply_bitcast_fusion
  732.8 2.2 copy.63
  735.3 2.0 fusion
  737.4 0.7 dynamic-slice_bitcast_fusion
  738.2 242.0 %reduce-scatter.3.cloned.1.call-done = f32[27,128,4]{1,0,2:T(8,128)} async-done(((f32[27,128,128]{1,0,2:T(8,128)}), f32[27,128,4]{1,0,2:T(8,128)}) %reduce-scatter.3.cloned.1.call-update) | async-done | bytes 55312 | tf_op jit(solution)/shard_map/reduce_scatter | solution.py:245
  980.2 245.7 %reduce-scatter.5.cloned.1.call-done = f32[27,128,4]{1,0,2:T(8,128)} async-done(((f32[27,128,128]{1,0,2:T(8,128)}), f32[27,128,4]{1,0,2:T(8,128)}) %reduce-scatter.5.cloned.1.call-update) | async-done | bytes 55312 | tf_op jit(solution)/shard_map/reduce_scatter | solution.py:240
  1226.1 0.7 fusion.65
  1226.8 2.7 copy.68
  1229.4 266.0 %all-reduce.15.cloned.1.call-done = (f32[27,128,4]{1,0,2:T(8,128)}, f32[27,128,4]{1,0,2:T(8,128)}) async-done(((f32[27,128,4]{1,0,2:T(8,128)}, f32[27,128,4]{1,0,2:T(8,128)}), (f32[27,128,4]{1,0,2:T(8,128)}, f32[27,128,4]{1,0,2:T(8,128)})) %all-reduce.15.cloned.1.call-update) | async-done | bytes 110608 | tf_op jit(solution)/shard_map/psum | solution.py:246
  1495.4 1.5 copy.66
  1496.9 1.5 copy.67
  (195 shorter events, 8.2 us)
Async XLA Ops:
  8.0 125.6 %copy-start = (bf16[27,512,16]{1,2,0:T(8,128)(2,1)S(1)}, bf16[27,512,16]{1,2,0:T(8,128)(2,1)}, u32[]{:S(2)}) copy-start(bf16[27,512,16]{1,2,0:T(8,128)(2,1)} %param.16) | copy-start | bytes 1327108
  8.0 123.1 %copy-start.9 = (bf16[27,128,128]{2,1,0:T(8,128)(2,1)S(1)}, bf16[27,128,128]{2,1,0:T(8,128)(2,1)}, u32[]{:S(2)}) copy-start(bf16[27,128,128]{2,1,0:T(8,128)(2,1)} %param.14) | copy-start | bytes 2654212
  8.0 698.3 %all-reduce.13.cloned.1.call-start = ((), (), s32[]{:S(2)}) async-start(), calls=%async_computation.5 | async-start | bytes 1310720 | tf_op jit(solution)/shard_map/psum | solution.py:212
  9.8 125.6 %collective-permute-start.1 = (bf16[1,8,32,128]{3,2,1,0:T(8,128)(2,1)}, bf16[1,8,32,128]{3,2,1,0:T(8,128)(2,1)}, u32[]{:S(2)}, u32[]{:S(2)}) collective-permute-start(bf16[1,8,32,128]{3,2,1,0:T(8,128)(2,1)} %get-tuple-element.38), channel_id=1, source_target_pairs={{1,0},{2,1},{3,2},{4,3},{5,4},{6,5},{7,6},{8,7},{9,8},{10,9},{11,1... | collective-permute-start | bytes 196616 | tf_op jit(solution)/shard_map/ppermute | solution.py:17
  11.1 124.3 %collective-permute-start = (bf16[1,8,32,128]{3,2,1,0:T(8,128)(2,1)}, bf16[1,8,32,128]{3,2,1,0:T(8,128)(2,1)}, u32[]{:S(2)}, u32[]{:S(2)}) collective-permute-start(bf16[1,8,32,128]{3,2,1,0:T(8,128)(2,1)} %get-tuple-element.37), channel_id=1, source_target_pairs={{0,1},{1,2},{2,3},{3,4},{4,5},{5,6},{6,7},{7,8},{8,9},{9,10},{10,1... | collective-permute-start | bytes 196616 | tf_op jit(solution)/shard_map/ppermute | solution.py:16
  18.7 113.3 %copy-start.35 = (s32[1,3]{1,0:T(1,128)S(1)}, s32[1,3]{1,0:T(1,128)}, u32[]{:S(2)}) copy-start(s32[1,3]{1,0:T(1,128)} %param.13) | copy-start | bytes 40
  18.7 113.3 %copy-start.36 = (f32[1,3]{1,0:T(1,128)S(1)}, f32[1,3]{1,0:T(1,128)}, u32[]{:S(2)}) copy-start(f32[1,3]{1,0:T(1,128)} %constant.67) | copy-start | bytes 40
  130.0 2.0 copy-start.13
  136.3 1.8 copy-start.7
  136.6 2.0 copy-start.6
  137.9 1.2 copy-start.10
  138.6 2.4 copy-start.33
  141.1 6.5 collective-permute-start.3
  142.4 5.2 collective-permute-start.2
  252.0 5.7 copy-start.14
  255.4 724.8 %reduce-scatter.3.cloned.1.call-start = ((), (), s32[]{:S(2)}) async-start(), calls=%async_computation.2 | async-start | bytes 2162688 | tf_op jit(solution)/shard_map/reduce_scatter | solution.py:245
  708.1 12.9 collective-permute-start.5
  709.4 11.6 collective-permute-start.4
  715.6 2.6 copy-start.2
  715.6 4.0 copy-start.1
  719.6 4.1 copy-start.34
  721.1 5.1 copy-start.11
  721.1 5.2 copy-start.3
  722.5 4.2 copy-start.4
  722.9 0.8 copy-start.12
  726.1 1.3 copy-start.5
  728.5 2.6 copy-start.32
  728.6 2.6 copy-start.31
  728.6 2.6 copy-start.30
  728.6 2.6 copy-start.29
  728.6 2.6 copy-start.28
  728.6 2.6 copy-start.27
  728.6 2.7 copy-start.26
  728.6 2.7 copy-start.25
  728.6 2.7 copy-start.24
  728.6 2.7 copy-start.23
  728.6 2.7 copy-start.22
  728.7 2.7 copy-start.21
  728.7 2.8 copy-start.20
  728.7 2.8 copy-start.19
  728.7 2.8 copy-start.18
  728.7 2.8 copy-start.17
  731.1 494.9 %reduce-scatter.5.cloned.1.call-start = ((), (), s32[]{:S(2)}) async-start(), calls=%async_computation.3 | async-start | bytes 2162688 | tf_op jit(solution)/shard_map/reduce_scatter | solution.py:240
  732.8 2.5 copy-start.15
  735.0 491.7 %all-reduce.11.cloned.1.call-start = ((), (), s32[]{:S(2)}) async-start(), calls=%async_computation.4 | async-start | bytes 2097152 | tf_op jit(solution)/shard_map/psum | solution.py:246
  735.2 2.8 copy-start.16
  735.3 490.8 %copy-start.8 = (f32[2,8,32,128]{3,2,1,0:T(8,128)S(1)}, f32[2,8,32,128]{3,2,1,0:T(8,128)}, u32[]{:S(2)}) copy-start(f32[2,8,32,128]{3,2,1,0:T(8,128)} %get-tuple-element.95) | copy-start | bytes 786436
  737.3 758.1 %all-reduce.15.cloned.1.call-start = ((), (), s32[]{:S(2)}) async-start(), calls=%async_computation.6 | async-start | bytes 262144 | tf_op jit(solution)/shard_map/psum | solution.py:246
  (1 other events, 0.7 us)
Sparse Core Ops, SparseCore 0:
  255.5 450.7 all-reduce.12
  731.2 249.0 reduce-scatter.2
  983.3 242.6 reduce-scatter.4
Sparse Core Ops, SparseCore 1:
  738.7 294.2 all-reduce.10
  1226.1 269.2 all-reduce.14
where the time goes:
time: 1510 us
  waiting for transfers between devices  1200 us (79%)
  blocking collectives  211 us (14%)
  local copies, waits for them, and re-layouts  31.2 us (2%)
  matrix products  20.4 us (1%)
  starting transfers between devices  17.9 us (1%)
  between operations  16.3 us (1%)
    psum x1, waiting for transfers between devices, body(): expanded_all = lax.psum(project(level_c, lower_rows), 'gx')  449 us
    psum x2, waiting for transfers between devices, body(): lax.psum((weight_a_part, weight_b_part, weight_c_term), 'member')  266 us
    reduce_scatter x1, waiting for transfers between devices, body(): lax.psum_scatter(weight_b_term, 'gx', scatter_dimension=2, tiled=True)  246 us
    reduce_scatter x1, waiting for transfers between devices, body(): lax.psum_scatter(weight_a_term, 'gx', scatter_dimension=2, tiled=True)  242 us
    all_gather x1, blocking collectives, body(): grad_planes = lax.all_gather(grad_halves, 'gx', axis=0, tiled=True)  110 us
    all_gather x1, blocking collectives, body(): planes_b = lax.all_gather(halves_b, 'gx', axis=0, tiled=True)  101 us
  transfers between devices with their start and end apart: 11, of which 4 were waited for; matrix products, arithmetic and copies ran while one was open for 2% of the time, Pallas kernels for 0%

commit v1 on v0

v1 whole, which is shorter than its diff:
```python
import jax
import jax.numpy as jnp
from jax import lax
from jax.experimental import pallas as pl
from jax.experimental.pallas import tpu as pltpu
from jax.sharding import PartitionSpec as P

f32 = jnp.float32
bf16 = jnp.bfloat16
MESH = pl.DeviceIdType.MESH

NY, NZH, NCORE, NXC, NZL = 4, 2, 2, 4, 8
NZ = NZH * NZL
SURVIVAL = (0.9, 0.8, 0.7)

COPIES = dict(
    halo_a=2,
    halo_b=2,
    halo_d=2,
    bz=7,
    bx=3,
    fz=7,
    fx=3,
    cot=4,
    cot_f=3,
    hid=4,
    hid_f=3,
    hb=7,
    gb=7,
    m1=7,
    rxb=3,
    rxf=3,
    rzb=7,
    rzf=7,
    a_x=3,
    a_z=15,
    a_all=7,
    b_x=3,
    b_z=15,
    b_all=7,
    c_core=1,
    c_y=3,
    c_zh=1,
    c_ay=3,
    c_ac=1,
)


class S:
    pass


TOTAL = 0
for _name, _count in COPIES.items():
    setattr(S, _name, TOTAL)
    TOTAL += _count
KINDS = ((S.a_x, S.a_z, S.a_all), (S.b_x, S.b_z, S.b_all))

NN = (((1,), (0,)), ((), ()))
NT = (((1,), (1,)), ((), ()))
TN = (((0,), (0,)), ((), ()))


def mm(a, b, dims=NN):
    return lax.dot_general(a, b, dims, preferred_element_type=f32)


def silu(v):
    return v * jax.nn.sigmoid(v)


def slope(v):
    s = jax.nn.sigmoid(v)
    return s * (1.0 + v * (1.0 - s))


SCRATCH = dict(
    fv=((2, 8, 32, 128), bf16),
    cv=((2, 8, 32, 128), bf16),
    kv=((1, 3), jnp.int32),
    wa=((9, 384, 128), bf16),
    wb=((9, 384, 128), bf16),
    wc=((432, 512), bf16),
    l1=((128, 128), bf16),
    l2=((128, 512), bf16),
    w2=((512, 128), bf16),
    w1=((128, 128), bf16),
    rv=((2, 8, 32, 128), bf16),
    halo_a=((2, 8, 32, 128), bf16),
    hraw=((8, 4, 8, 32, 128), bf16),
    hs=((8, 3, 4, 10, 32, 128), bf16),
    la=((2, 256, 128), f32),
    pool_s=((128, 128), f32),
    grow_s=((128, 128), f32),
    hb_own=((64, 128), bf16),
    halo_b=((2, 64, 128), bf16),
    hbraw=((8, 3, 64, 128), bf16),
    hsb=((8, 3, 3, 6, 16, 128), bf16),
    small_s=((32, 128), f32),
    gd_own=((64, 128), bf16),
    halo_d=((2, 64, 128), bf16),
    bz_buf=((8, 16, 128), bf16),
    ge=((18, 16, 128), bf16),
    fz_buf=((8, 16, 128), bf16),
    fx_buf=((4, 4, 16, 128), bf16),
    st=((448, 256), bf16),
    mp=((18, 16, 128), bf16),
    up=((16, 16, 128), bf16),
    rxb=((3, 6, 16, 128), bf16),
    rxf=((3, 4, 16, 128), bf16),
    sb=((6, 16, 128), bf16),
    sf=((4, 16, 128), bf16),
    rzb=((7, 2, 16, 128), bf16),
    rzf=((7, 16, 128), bf16),
    gbs=((3, 3, 6, 16, 128), bf16),
    cq=((8, 128, 512), bf16),
    gbq=((8, 64, 128), bf16),
    m1q=((8, 64, 128), bf16),
    gt=((8, 128, 512), bf16),
    xs=((2, 4, 4, 32, 128), bf16),
    xr=((2, 3, 4, 32, 128), bf16),
    zs=((2, 8, 16, 128), bf16),
    zr=((2, 16, 16, 128), bf16),
    zt=((2, 16, 128), f32),
    c_own=((224, 128), bf16),
    dc=((2, 4, 224, 128), bf16),
    c_cr=((4, 224, 128), bf16),
    c_ys=((4, 224, 128), bf16),
    c_yr=((3, 224, 128), bf16),
    c_zs=((224, 128), bf16),
    c_zr=((224, 128), bf16),
)


class Bufs:
    pass


def kernel(
    feat_h,
    cot_h,
    keep_h,
    wa_h,
    wb_h,
    wc_h,
    l1_h,
    l2_h,
    w2_h,
    w1_h,
    res,
    fga,
    fgb,
    fgc,
    *scratch,
):
    b = Bufs()
    for name, ref in zip(SCRATCH, scratch):
        setattr(b, name, ref)
    local_sem, send_sem, recv_sem = scratch[len(SCRATCH) :]

    m = lax.axis_index("member")
    g = lax.axis_index("gx")
    x, z = g // NZL, g % NZL
    core, zh, y = m % NCORE, (m // NCORE) % NZH, m // (NCORE * NZH)
    z16 = zh * NZL + z
    q = y * 2 + core

    def dev(dy=None, dzh=None, dcore=None, dx=None, dz=None):
        yy = y if dy is None else dy
        hh = zh if dzh is None else dzh
        cc = core if dcore is None else dcore
        xx = x if dx is None else dx
        zz = z if dz is None else dz
        return ((yy * NZH + hh) * NCORE + cc, xx * NZL + zz)

    nxt = (m, (g + 1) % (NXC * NZL))
    prv = (m, (g + NXC * NZL - 1) % (NXC * NZL))
    x_of = [(x + k) % NXC for k in range(NXC)]
    z_of = [(z + k) % NZL for k in range(NZL)]
    y_of = [(y + k) % NY for k in range(NY)]
    y_from = [(y + NY - k) % NY for k in range(NY)]
    z16_of = [(z16 + k) % NZ for k in range(NZ)]
    group_of = [(y_of[k // 2], (core + k) % 2) for k in range(8)]
    group_dev = [dev(dy=yy, dcore=cc) for yy, cc in group_of]
    sibling = dev(dcore=1 - core)

    barrier = pltpu.get_barrier_semaphore()
    targets = [prv, nxt]
    targets += [dev(dx=x_of[k]) for k in range(1, NXC)]
    targets += [dev(dzh=z16_of[k] // NZL, dz=z16_of[k] % NZL) for k in range(1, NZ)]
    targets += group_dev[1:]
    for target in targets:
        pl.semaphore_signal(barrier, inc=1, device_id=target, device_id_type=MESH)

    started = []

    def finish(count):
        for copy in started[:count]:
            copy.wait_send()
        del started[:count]

    def send(name, k, src, dst, target):
        index = name + k
        copy = pltpu.make_async_remote_copy(
            src_ref=src,
            dst_ref=dst,
            send_sem=send_sem.at[index],
            recv_sem=recv_sem.at[index],
            device_id=target,
            device_id_type=MESH,
        )
        copy.start()
        started.append(copy)
        return copy

    def arrived(copies):
        for copy in copies:
            copy.wait_recv()

    loads = Bufs()

    def load_all(first, **sources):
        for k, (name, src) in enumerate(sources.items()):
            load = pltpu.make_async_copy(src, getattr(b, name), local_sem.at[first + k])
            load.start()
            setattr(loads, name, load)

    load_all(0, fv=feat_h.at[0], wa=wa_h)
    pl.semaphore_wait(barrier, len(targets))
    halo_a_copies = [
        send(S.halo_a, 0, feat_h.at[0, 1], b.halo_a.at[0], nxt),
        send(S.halo_a, 1, feat_h.at[0, 0], b.halo_a.at[1], prv),
    ]
    load_all(2, cv=cot_h.at[0], w1=w1_h, kv=keep_h, l1=l1_h, wb=wb_h, w2=w2_h, wc=wc_h, l2=l2_h)

    has_prev = (g > 0).astype(f32)
    has_next = (g < NXC * NZL - 1).astype(f32)

    def z_shifts(h, length):
        rows = h.shape[0]
        pos = lax.broadcasted_iota(jnp.int32, h.shape, 0) % length
        before = jnp.where(pos == 0, 0.0, pltpu.roll(h, 1, 0))
        after = jnp.where(pos == length - 1, 0.0, pltpu.roll(h, rows - 1, 0))
        return before, h, after

    def put(cat, plane, h, grid_y, grid_z):
        for k, piece in enumerate(z_shifts(h, grid_z)):
            cat[k, plane, 1 : 1 + grid_y] = piece.astype(bf16).reshape(grid_y, grid_z, 128)

    def pool_yz(v, grid_y, grid_z, scratch_ref):
        half = v.reshape(grid_y // 2, 2, grid_z, 128).sum(axis=1)
        n = grid_y // 2 * grid_z
        scratch_ref[0:n, :] = half.reshape(n, 128)
        even = scratch_ref[pl.ds(0, n // 2, stride=2), :]
        return even + scratch_ref[pl.ds(1, n // 2, stride=2), :]

    def grow_yz(v, grid_y, grid_z, scratch_ref):
        n = grid_y * grid_z
        scratch_ref[pl.ds(0, n, stride=2), :] = v
        scratch_ref[pl.ds(1, n, stride=2), :] = v
        wide = scratch_ref[0 : 2 * n, :].reshape(grid_y, 1, 2 * grid_z, 128)
        return jnp.broadcast_to(wide, (grid_y, 2, 2 * grid_z, 128)).reshape(4 * n, 128)

    def wide_field(cat, plane, first, grid_y, grid_z, turned=False):
        order = (2, 1, 0) if turned else (0, 1, 2)
        pieces = [
            cat[k, plane, first : first + grid_y].reshape(grid_y * grid_z, 128) for k in order
        ]
        return jnp.concatenate(pieces, axis=1)

    row = lax.broadcasted_iota(jnp.int32, (128, 128), 0)
    col = lax.broadcasted_iota(jnp.int32, (128, 128), 1)
    unit = (row == col).astype(f32).astype(bf16)

    def clear(i, carry):
        for k in range(3):
            for p in range(4):
                b.hs[i, k, p, 0] = jnp.zeros((32, 128), bf16)
                b.hs[i, k, p, 9] = jnp.zeros((32, 128), bf16)
            for p in range(3):
                b.hsb[i, k, p, 0] = jnp.zeros((16, 128), bf16)
                b.hsb[i, k, p, 5] = jnp.zeros((16, 128), bf16)
        return carry

    clear(q, 0)
    for ref in (b.ge, b.mp):
        ref[0] = jnp.zeros((16, 128), bf16)
        ref[17] = jnp.zeros((16, 128), bf16)

    hs_own = b.hs.at[q]
    hsb_own = b.hsb.at[q]

    def put_a(plane, h):
        put(hs_own, plane, h, 8, 32)
        b.hraw[q, plane] = h.astype(bf16).reshape(8, 32, 128)

    loads.fv.wait()
    for p in range(2):
        put_a(1 + p, silu(b.fv[p].astype(f32).reshape(256, 128)))

    def taps_a(acc, p, dx):
        for dy in range(3):
            acc = acc + mm(wide_field(hs_own, p + dx, dy, 8, 32), b.wa[3 * dx + dy])
        return acc

    loads.wa.wait()
    acc_a = [jnp.zeros((256, 128), f32), jnp.zeros((256, 128), f32)]
    acc_a[0] = taps_a(taps_a(acc_a[0], 0, 1), 0, 2)
    acc_a[1] = taps_a(taps_a(acc_a[1], 1, 1), 1, 0)
    for p in range(2):
        b.la[p] = acc_a[p]

    loads.cv.wait()
    loads.w1.wait()
    loads.kv.wait()
    flags = b.kv[...].astype(f32)
    flag = [flags[0:1, j : j + 1] for j in range(3)]
    scale = [flag[j] * f32(1.0 / SURVIVAL[j]) for j in range(3)]
    up32 = [b.cv[p].astype(f32).reshape(256, 128) for p in range(2)]
    grad_e1 = pool_yz(up32[0] + up32[1], 8, 32, b.pool_s).astype(bf16)
    grad_d = mm(grad_e1, b.w1[...], NT).astype(bf16)
    b.gd_own[...] = grad_d
    b.bz_buf[z] = pool_yz(grad_d.astype(f32), 4, 16, b.small_s).astype(bf16)
    bz_copies = [
        send(S.bz, k - 1, b.bz_buf.at[z], b.bz_buf.at[z], dev(dz=z_of[k]))
        for k in range(1, NZL)
    ]
    halo_d_copies = [
        send(S.halo_d, 0, b.gd_own, b.halo_d.at[0], nxt),
        send(S.halo_d, 1, b.gd_own, b.halo_d.at[1], prv),
    ]
    for p in range(2):
        turned = mm(unit, (up32[p] * flag[0]).astype(bf16), NT).astype(bf16)
        b.cq[q, :, 256 * p : 256 * p + 256] = turned
    peers = [sibling] + [dev(dy=y_of[k]) for k in range(1, NY)]

    def whole(ref, slot, to_y):
        return ref.at[slot]

    def some(count):
        return lambda ref, slot, to_y: ref.at[slot, pl.ds(to_y // 2, count)]

    def spread(name, ref, part=whole):
        result = []
        for k in range(4):
            piece = part(ref, q, y_of[k])
            result.append(send(name, k, piece, piece, peers[k]))
        return result

    def forward(name, ref, copies, part=whole):
        result = []
        for k in range(1, NY):
            piece = part(ref, y_from[k] * 2 + core, y)
            pltpu.make_async_remote_copy(
                src_ref=piece,
                dst_ref=piece,
                send_sem=send_sem.at[0],
                recv_sem=recv_sem.at[copies[k]],
                device_id=sibling,
                device_id_type=MESH,
            ).wait_recv()
            result.append(send(name, k - 1, piece, piece, sibling))
        return result

    def to_group(name, ref, part=whole):
        result = []
        for k in range(1, 8):
            piece = part(ref, q, group_of[k][0])
            result.append(send(name, k - 1, piece, piece, group_dev[k]))
        return result

    cot_copies = spread(S.cot, b.cq)
    cot_sems = [S.cot + k for k in range(4)]
    hid_sems = [S.hid + k for k in range(4)]

    arrived(halo_a_copies)
    put_a(0, silu(b.halo_a[0].astype(f32).reshape(256, 128)) * has_prev)
    put_a(3, silu(b.halo_a[1].astype(f32).reshape(256, 128)) * has_next)
    hid_copies = spread(S.hid, b.hraw, some(3))
    acc_a[0] = taps_a(b.la[0], 0, 0)
    acc_a[1] = taps_a(b.la[1], 1, 2)
    level_a = []
    for p in range(2):
        value = b.fv[p].astype(f32).reshape(256, 128) + scale[0] * acc_a[p]
        b.la[p] = value
        level_a.append(value)
    pooled = (pool_yz(level_a[0] + level_a[1], 8, 32, b.pool_s) * 0.125).astype(bf16)
    loads.l1.wait()
    lb = mm(pooled, b.l1[...]).astype(bf16).astype(f32)

    hidden_b = silu(lb)
    b.hb_own[...] = hidden_b.astype(bf16)
    halo_b_copies = [
        send(S.halo_b, 0, b.hb_own, b.halo_b.at[0], nxt),
        send(S.halo_b, 1, b.hb_own, b.halo_b.at[1], prv),
    ]

    def put_b(plane, h):
        put(hsb_own, plane, h, 4, 16)
        b.hbraw[q, plane] = h.astype(bf16)

    put_b(1, hidden_b)

    arrived(bz_copies)
    for k in range(4):
        both = b.bz_buf[2 * k].astype(f32) + b.bz_buf[2 * k + 1].astype(f32)
        b.ge[1 + 4 * x + k] = both.astype(bf16)
    own_ge = b.ge.at[pl.ds(1 + 4 * x, 4)]
    bx_copies = [send(S.bx, k - 1, own_ge, own_ge, dev(dx=x_of[k])) for k in range(1, NXC)]

    def taps_b(acc, dx):
        for dy in range(3):
            acc = acc + mm(wide_field(hsb_own, dx, dy, 4, 16), b.wb[3 * dx + dy])
        return acc

    loads.wb.wait()
    acc_b = taps_b(jnp.zeros((64, 128), f32), 1)
    arrived(halo_b_copies)
    put_b(0, b.halo_b[0].astype(f32) * has_prev)
    put_b(2, b.halo_b[1].astype(f32) * has_next)
    acc_b = taps_b(taps_b(acc_b, 0), 2)
    level_b = lb + scale[1] * acc_b
    b.fz_buf[z] = (pool_yz(level_b, 4, 16, b.small_s) * 0.25).astype(bf16)
    fz_copies = [
        send(S.fz, k - 1, b.fz_buf.at[z], b.fz_buf.at[z], dev(dz=z_of[k]))
        for k in range(1, NZL)
    ]

    for k in range(3):
        for p in range(3):
            b.gbs[k, p, 0] = jnp.zeros((16, 128), bf16)
            b.gbs[k, p, 5] = jnp.zeros((16, 128), bf16)
    lax.fori_loop(1, 8, lambda k, carry: clear(lax.rem(q + k, 8), carry), 0)
    for load in (loads.w2, loads.wc, loads.l2):
        load.wait()
    arrived(bx_copies)
    grad_e2 = b.ge[1:17].reshape(256, 128)
    own_rows = b.w2[pl.ds(pl.multiple_of(g * 16, 16), 16), :]
    grad_t = mm(own_rows, grad_e2, NT).astype(bf16).astype(f32)
    lane = lax.broadcasted_iota(jnp.int32, (16, 256), 1)
    pos_p, pos_y, pos_z = lane // 16, (lane // 8) % 2, lane % 8

    def moved(v, pos, length, step, d):
        if d == 0:
            return v
        ok = (pos + d >= 0) & (pos + d < length)
        return jnp.where(ok, pltpu.roll(v, (-d * step) % 256, 1), 0.0)

    for dx in range(3):
        vx = moved(grad_t, pos_p, 16, 16, 1 - dx)
        for dy in range(3):
            vy = moved(vx, pos_y, 2, 8, 1 - dy)
            for dz in range(3):
                tap = 9 * dx + 3 * dy + dz
                b.st[16 * tap : 16 * tap + 16, :] = moved(vy, pos_z, 8, 1, 1 - dz).astype(bf16)
    b.st[432:448, :] = jnp.zeros((16, 256), bf16)
    back_part = mm(b.st[0:432, :], b.wc[...], TN)
    start = z // 2 + z % 2
    two_e2 = b.ge[pl.ds(4 * x + start, 2)].reshape(32, 128)
    two_c = mm(two_e2, b.w2[...], NT).astype(bf16)
    two_m2 = mm(two_c, b.l2[...], NT)

    arrived(fz_copies)
    for k in range(4):
        both = b.fz_buf[2 * k].astype(f32) + b.fz_buf[2 * k + 1].astype(f32)
        b.fx_buf[x, k] = (both * 0.5).astype(bf16)
    fx_copies = [
        send(S.fx, k - 1, b.fx_buf.at[x], b.fx_buf.at[x], dev(dx=x_of[k]))
        for k in range(1, NXC)
    ]
    hb_copies = to_group(S.hb, b.hbraw, some(2))
    cot_forward = forward(S.cot_f, b.cq, cot_sems)
    arrived(fx_copies)
    pooled_two = b.fx_buf[...].reshape(256, 128)
    lc_b = mm(pooled_two, b.l2[...]).astype(bf16)
    lc = lc_b.astype(f32)
    sig = jax.nn.sigmoid(lc)
    hidden_c = (lc * sig).astype(bf16)
    weighted = (scale[2] * (sig * (1.0 + lc * (1.0 - sig))) * back_part).astype(bf16)
    b.mp[1:17] = mm(weighted, b.l2[...], NT).astype(bf16).reshape(16, 16, 128)
    rxb_copies = [
        send(S.rxb, k - 1, b.mp.at[pl.ds(4 * x_of[k], 6)], b.rxb.at[k - 1], dev(dx=x_of[k]))
        for k in range(1, NXC)
    ]
    taps = mm(b.wc[...], hidden_c, NT).reshape(9, 3, 16, 256)

    def folded(v, pos, length, step):
        total = v[:, 1]
        for d in (-1, 1):
            ok = (pos + d >= 0) & (pos + d < length)
            piece = v[:, 1 + d]
            turned = pltpu.roll(piece.reshape(-1, 256), (-d * step) % 256, 1)
            total = total + jnp.where(ok[None], turned.reshape(piece.shape), 0.0)
        return total

    conv_t = folded(taps, pos_z, 8, 1).reshape(3, 3, 16, 256)
    conv_t = folded(conv_t, pos_y, 2, 8).reshape(1, 3, 16, 256)
    conv_t = folded(conv_t, pos_p, 16, 16).reshape(16, 256)
    row16 = lax.broadcasted_iota(jnp.int32, (16, 512), 0)
    lane16 = lax.broadcasted_iota(jnp.int32, (16, 512), 1)
    pick = (lane16 == row16 + g * 16).astype(f32).astype(bf16)
    own_lc = mm(pick, lc_b, NT)
    level_c = (own_lc + scale[2] * conv_t).astype(bf16)
    b.up[...] = mm(level_c, own_rows, TN).astype(bf16).reshape(16, 16, 128)
    rxf_copies = [
        send(S.rxf, k - 1, b.up.at[pl.ds(4 * x_of[k], 4)], b.rxf.at[k - 1], dev(dx=x_of[k]))
        for k in range(1, NXC)
    ]

    arrived(rxb_copies)
    both = b.mp[pl.ds(4 * x, 6)].astype(f32)
    for k in range(3):
        both = both + b.rxb[k].astype(f32)
    b.sb[...] = both.astype(bf16)
    rzb_copies = []
    for k in range(1, NZL):
        first = z_of[k] // 2 + z_of[k] % 2
        rzb_copies.append(
            send(S.rzb, k - 1, b.sb.at[pl.ds(first, 2)], b.rzb.at[k - 1], dev(dz=z_of[k]))
        )
    arrived(rxf_copies)
    both = b.up[pl.ds(4 * x, 4)].astype(f32)
    for k in range(3):
        both = both + b.rxf[k].astype(f32)
    b.sf[...] = both.astype(bf16)
    rzf_copies = [
        send(S.rzf, k - 1, b.sf.at[z_of[k] // 2], b.rzf.at[k - 1], dev(dz=z_of[k]))
        for k in range(1, NZL)
    ]

    grad_w = (scale[2] * mm(b.st[...], hidden_c)).astype(bf16)
    for cc in range(2):
        for yy in range(NY):
            b.dc[cc, yy] = grad_w[224 * cc : 224 * cc + 224, 128 * yy : 128 * yy + 128]
    hid_forward = forward(S.hid_f, b.hraw, hid_sems, some(3))
    c_core = send(S.c_core, 0, b.dc.at[1 - core], b.c_cr, sibling)

    def prepare(slot):
        def one(p, carry):
            put(b.hs.at[slot], p, b.hraw[slot, p].astype(f32).reshape(256, 128), 8, 32)
            return carry

        lax.fori_loop(y // 2, y // 2 + 3, one, 0)

    hid_copies[0].wait_recv()
    prepare(y * 2 + 1 - core)
    for k in range(1, NY):
        prepare(y_of[k] * 2 + core)

    c_core.wait_recv()
    for yy in range(NY):
        b.c_ys[yy] = (b.dc[core, yy].astype(f32) + b.c_cr[yy].astype(f32)).astype(bf16)
    c_y = [
        send(S.c_y, k - 1, b.c_ys.at[y_of[k]], b.c_yr.at[k - 1], dev(dy=y_of[k]))
        for k in range(1, NY)
    ]

    arrived(rzb_copies)
    both = b.sb[pl.ds(start, 2)].astype(f32)
    for k in range(7):
        both = both + b.rzb[k].astype(f32)
    two_m2 = (two_m2.reshape(2, 16, 128) + both).astype(bf16).astype(f32)
    even = (z % 2 == 0).astype(f32)
    lo, hi = two_m2[0], two_m2[1]
    own_m2 = hi * even + lo * (1.0 - even)
    arrived(halo_d_copies)

    def grad_plane(field, m2):
        return (field.astype(f32) + grow_yz(m2, 2, 8, b.small_s) * 0.125).astype(bf16)

    grad_b = grad_plane(b.gd_own[...], own_m2)
    grad_b32 = grad_b.astype(f32)
    b.gbq[q] = (grad_b32 * flag[1]).astype(bf16)
    gb_copies = to_group(S.gb, b.gbq)
    put(b.gbs, 1, grad_b32, 4, 16)
    put(b.gbs, 0, grad_plane(b.halo_d[0], lo).astype(f32) * has_prev, 4, 16)
    put(b.gbs, 2, grad_plane(b.halo_d[1], hi).astype(f32) * has_next, 4, 16)
    back_b = jnp.zeros((64, 128), f32)
    for t in range(9):
        dx, dy = t // 3, t % 3
        for dz in range(3):
            part = b.gbs[2 - dz, 2 - dx, 2 - dy : 6 - dy].reshape(64, 128)
            back_b = back_b + mm(part, b.wb[t, 128 * dz : 128 * dz + 128, :], NT)
    grad_p = (grad_b32 + scale[1] * slope(lb) * back_b).astype(bf16)
    grad_m1 = mm(grad_p, b.l1[...], NT).astype(bf16).astype(f32)
    b.m1q[q] = (grad_m1 * flag[0]).astype(bf16)
    m1_copies = to_group(S.m1, b.m1q)
    early = len(started)

    arrived(c_y)
    total = b.c_ys[y].astype(f32)
    for k in range(3):
        total = total + b.c_yr[k].astype(f32)
    b.c_zs[...] = total.astype(bf16)
    c_zh = send(S.c_zh, 0, b.c_zs, b.c_zr, dev(dzh=1 - zh))
    arrived(hb_copies)
    for k in range(1, 8):
        slot = group_of[k][0] * 2 + group_of[k][1]
        for p in range(2):
            plane = y // 2 + p
            put(b.hsb.at[slot], plane, b.hbraw[slot, plane].astype(f32), 4, 16)
    arrived(gb_copies)
    numbers = [jnp.minimum(4 * q + i, 26) for i in range(4)]
    where = [(t // 9, (t // 3) % 3, t % 3) for t in numbers]

    def keep_sum(kind, i, value):
        for k in range(NXC):
            b.xs[kind, k, i] = value[32 * k : 32 * k + 32].astype(bf16)

    def along_x(kind):
        return [
            send(
                KINDS[kind][0],
                k - 1,
                b.xs.at[kind, x_of[k]],
                b.xr.at[kind, k - 1],
                dev(dx=x_of[k]),
            )
            for k in range(1, NXC)
        ]

    source = ((row // 4) % 4) * 32 + (row // 16) * 4 + row % 4
    shuffle = (col == source).astype(f32).astype(bf16)

    def along_z(kind):
        total = b.xs[kind, x].astype(f32)
        for k in range(3):
            total = total + b.xr[kind, k].astype(f32)
        pieces = mm(shuffle, total.astype(bf16).reshape(128, 128)).astype(bf16)
        b.zs[kind] = pieces.reshape(8, 16, 128)
        copies = []
        for k in sorted(range(1, NZ), key=lambda k: abs(k - NZ // 2)):
            target = dev(dzh=z16_of[k] // NZL, dz=z16_of[k] % NZL)
            src = b.zs.at[kind, z16_of[k] % NZL]
            copies.append(send(KINDS[kind][1], k - 1, src, b.zr.at[kind, z16], target))
        b.zr[kind, z16] = b.zs[kind, z]
        return copies

    def to_all(kind):
        total = b.zr[kind, 0].astype(f32)
        for k in range(1, NZ):
            total = total + b.zr[kind, k].astype(f32)
        b.zt[kind] = total
        own = (fga, fgb)[kind].at[q]
        copies = [
            send(KINDS[kind][2], k - 1, b.zt.at[kind], own, group_dev[k]) for k in range(1, 8)
        ]
        stores.append(pltpu.make_async_copy(b.zt.at[kind], own, local_sem.at[11 + kind]))
        stores[-1].start()
        return copies

    turned_b = mm(unit, b.gbq[...].reshape(512, 128), NT).astype(bf16)
    for i, (dx, dy, dz) in enumerate(where):
        field = b.hsb[:, dz, dx, pl.ds(dy, 4)].reshape(512, 128)
        keep_sum(1, i, mm(turned_b, field) * f32(1.0 / SURVIVAL[1]))
    b_x = along_x(1)
    arrived(rzf_copies)
    both = b.sf[z // 2].astype(f32)
    for k in range(7):
        both = both + b.rzf[k].astype(f32)
    level_d = (level_b + grow_yz(both, 2, 8, b.small_s)).astype(bf16)
    wide = grow_yz(mm(level_d, b.w1[...]), 4, 16, b.grow_s)
    for p in range(2):
        b.rv[p] = (b.la[p] + wide).astype(bf16).reshape(8, 32, 128)
    stores = [pltpu.make_async_copy(b.rv, res.at[0], local_sem.at[10])]
    stores[0].start()
    for k in range(1, NY):
        hid_forward[k - 1].wait_recv()
        prepare(y_from[k] * 2 + 1 - core)
    arrived(b_x)
    b_z = along_z(1)
    cot_copies[0].wait_recv()
    arrived(cot_forward)

    coarse = lax.broadcasted_iota(jnp.int32, (64, 512), 0)
    fine = lax.broadcasted_iota(jnp.int32, (64, 512), 1)
    above = ((fine // 64) % 4) * 16 + (fine % 32) // 2
    grow = jnp.where(coarse == above, 0.125, 0.0).astype(bf16)
    arrived(m1_copies)
    for j in range(8):
        b.gt[j] = (b.cq[j].astype(f32) + mm(b.m1q[j], grow, TN)).astype(bf16)
    for pair in range(2):
        acc = jnp.zeros((128, 256), f32)
        for j in range(8):
            pieces = []
            for i in (2 * pair, 2 * pair + 1):
                dx, dy, dz = where[i]
                pieces.append(b.hs[j, dz, pl.ds(dx, 2), pl.ds(dy, 8)].reshape(512, 128))
            acc = acc + mm(b.gt[j], jnp.concatenate(pieces, axis=1))
        acc = acc * f32(1.0 / SURVIVAL[0])
        keep_sum(0, 2 * pair, acc[:, 0:128])
        keep_sum(0, 2 * pair + 1, acc[:, 128:256])
    a_x = along_x(0)

    arrived(b_z)
    b_all = to_all(1)
    arrived(a_x)
    a_z = along_z(0)
    finish(early)
    c_zh.wait_recv()
    b.c_own[...] = (b.c_zs[...].astype(f32) + b.c_zr[...].astype(f32)).astype(bf16)
    rows_c = pl.ds(pl.multiple_of(core * 224, 16), 224)
    lanes_y = pl.ds(pl.multiple_of(y * 128, 128), 128)
    own_c = fgc.at[rows_c, lanes_y]
    c_ay = [send(S.c_ay, k - 1, b.c_own, own_c, dev(dy=y_of[k])) for k in range(1, NY)]
    stores.append(pltpu.make_async_copy(b.c_own, own_c, local_sem.at[13]))
    stores[-1].start()
    arrived(a_z)
    a_all = to_all(0)
    arrived(c_ay)
    for copy in stores:
        copy.wait()
    half_c = fgc.at[rows_c]
    c_ac = send(S.c_ac, 0, half_c, half_c, sibling)
    finish(len(started) - 8)
    arrived(b_all)
    arrived(a_all)
    c_ac.wait_recv()
    finish(len(started))


def finalize(
    res, fga, fgb, fgc, out, out_a, out_b, out_c, res_v, fg_v, fgc_v, tables, wide, sems
):
    loads = [
        pltpu.make_async_copy(fgc, fgc_v, sems.at[0]),
        pltpu.make_async_copy(fga, fg_v.at[0], sems.at[1]),
        pltpu.make_async_copy(fgb, fg_v.at[1], sems.at[2]),
        pltpu.make_async_copy(res, res_v, sems.at[9]),
    ]
    copies = [pltpu.make_async_copy(res_v, out, sems.at[3])]
    for load in loads:
        load.start()
    loads[3].wait()
    copies[0].start()
    for kind, target in enumerate((out_a, out_b)):
        loads[1 + kind].wait()
        for t in range(27):
            first = 4 * (t % 4)
            tables[kind, t] = fg_v[kind, t // 4, first : first + 4]
        copies.append(pltpu.make_async_copy(tables.at[kind], target, sems.at[4 + kind]))
        copies[-1].start()
    loads[0].wait()
    for part in range(3):
        rows = pl.ds(144 * part, 144)
        wide[rows] = fgc_v[rows].astype(f32)
        copies.append(pltpu.make_async_copy(wide.at[rows], out_c.at[rows], sems.at[6 + part]))
        copies[-1].start()
    for copy in copies:
        copy.wait()


def body(
    features,
    cotangent,
    keep_flags,
    conv_a,
    conv_b,
    conv_c,
    lift_one,
    lift_two,
    lower_two,
    lower_one,
):
    hbm = pl.BlockSpec(memory_space=pltpu.HBM)
    result, fga, fgb, fgc = pl.pallas_call(
        kernel,
        out_shape=(
            jax.ShapeDtypeStruct(features.shape, bf16),
            jax.ShapeDtypeStruct((8, 16, 128), f32),
            jax.ShapeDtypeStruct((8, 16, 128), f32),
            jax.ShapeDtypeStruct((448, 512), bf16),
        ),
        in_specs=[hbm] * 10,
        out_specs=(hbm,) * 4,
        scratch_shapes=[pltpu.VMEM(shape, dtype) for shape, dtype in SCRATCH.values()]
        + [
            pltpu.SemaphoreType.DMA((14,)),
            pltpu.SemaphoreType.DMA((TOTAL,)),
            pltpu.SemaphoreType.DMA((TOTAL,)),
        ],
        compiler_params=pltpu.CompilerParams(
            collective_id=0, has_side_effects=True, vmem_limit_bytes=60 * 1024 * 1024
        ),
        cost_estimate=pl.CostEstimate(
            flops=1_400_000_000, bytes_accessed=5_000_000, transcendentals=600_000
        ),
    )(
        features,
        cotangent,
        keep_flags,
        conv_a.reshape(9, 384, 128),
        conv_b.reshape(9, 384, 128),
        conv_c.transpose(0, 2, 1).reshape(432, 512),
        lift_one,
        lift_two,
        lower_two,
        lower_one,
    )

    result, grad_a, grad_b, grad_c = pl.pallas_call(
        finalize,
        out_shape=(
            jax.ShapeDtypeStruct(features.shape, bf16),
            jax.ShapeDtypeStruct((27, 4, 128), f32),
            jax.ShapeDtypeStruct((27, 4, 128), f32),
            jax.ShapeDtypeStruct((432, 512), f32),
        ),
        in_specs=[hbm] * 4,
        out_specs=(hbm,) * 4,
        scratch_shapes=[
            pltpu.VMEM(features.shape, bf16),
            pltpu.VMEM((2, 8, 16, 128), f32),
            pltpu.VMEM((448, 512), bf16),
            pltpu.VMEM((2, 27, 4, 128), f32),
            pltpu.VMEM((432, 512), f32),
            pltpu.SemaphoreType.DMA((10,)),
        ],
        compiler_params=pltpu.CompilerParams(vmem_limit_bytes=60 * 1024 * 1024),
    )(result, fga, fgb, fgc)
    return (
        result,
        grad_a.transpose(0, 2, 1),
        grad_b.transpose(0, 2, 1),
        grad_c.reshape(27, 16, 512).transpose(0, 2, 1),
    )


def solution(mesh):
    return jax.shard_map(
        body,
        mesh=mesh,
        in_specs=(
            P("member", "gx", None, None, None),
            P("member", "gx", None, None, None),
            P("member", None),
            P(),
            P(),
            P(None, None, "gx"),
            P(),
            P(),
            P(),
            P(),
        ),
        out_specs=(
            P("member", "gx", None, None, None),
            P(None, None, "gx"),
            P(None, None, "gx"),
            P(None, None, "gx"),
        ),
        check_vma=False,
    )
```

time: 1510 us -> 87.4 us (0.06)
  waiting for transfers between devices: 1200 us -> 0 us
  blocking collectives: 211 us -> 0 us
  Pallas kernels: 0 us -> 86.6 us
  local copies, waits for them, and re-layouts: 31.2 us -> 0 us
  matrix products: 20.4 us -> 0 us
  starting transfers between devices: 17.9 us -> 0 us
  between operations: 16.3 us -> 0.64 us
    psum x3 -> x0, waiting for transfers between devices: 715 us -> none  [the longest x1 449 us: body(): expanded_all = lax.psum(project(level_c, lower_rows), 'gx')]
    reduce_scatter x2 -> x0, waiting for transfers between devices: 488 us -> none  [the longest x1 246 us: body(): lax.psum_scatter(weight_b_term, 'gx', scatter_dimension=2, tiled=True)]
    all_gather x2 -> x0, blocking collectives: 211 us -> none  [the longest x1 110 us: body(): grad_planes = lax.all_gather(grad_halves, 'gx', axis=0, tiled=True)]
    pallas_call x0 -> x2, Pallas kernels: none -> 86.6 us  [the longest x1 84.5 us: body(): pl.pallas_call(kernel, out_shape=(jax.ShapeDtypeStruct(features.shape, bf...]
    dot_general x21 -> x0, matrix products: 20.4 us -> none  [the longest x16 15.8 us: project(): jnp.dot(flatten(field_in), matrix, preferred_element_type=jnp.float32)]
    ppermute x6 -> x0, starting transfers between devices: 17.7 us -> none  [the longest x3 13.9 us: extended(): before = lax.ppermute(last, axis, up)]
  transfers between devices with their start and end apart: 11 -> 0, of which waited for: 4 -> 0; matrix products, arithmetic and copies ran while one was open for 2% -> 0% of each run, Pallas kernels for 0% -> 0%
where the time goes in v1:
time: 87.4 us; the launch traced here: 87.3 us
  Pallas kernels  86.6 us (99%)
    pallas_call x1, Pallas kernels, body(): pl.pallas_call(kernel, out_shape=(jax.ShapeDtypeStruct(features.shape, bf...  84.5 us
    pallas_call x1, Pallas kernels, body(): pl.pallas_call(finalize, out_shape=(jax.ShapeDtypeStruct(features.shape,...  2.17 us

profile of v1, /device:TPU:1, one launch (start us, length us, event | category | flops | bytes accessed | tf_op | source)
XLA Modules:
  0.0 87.3 jit_solution(3422545670861290182)
XLA Ops:
  0.6 84.5 %shard_map.129 = (bf16[1,2,8,32,128]{4,3,2,1,0:T(8,128)(2,1)}, f32[8,16,128]{2,1,0:T(8,128)}, f32[8,16,128]{2,1,0:T(8,128)}, bf16[448,512]{1,0:T(8,128)(2,1)}) custom-call(bf16[1,2,8,32,128]{4,3,2,1,0:T(8,128)(2,1)} %feat_h.1, bf16[1,2,8,32,128]{4,3,2,1,0:T(8,128)(2,1)} %cot_h.1, s32[1,3]{1,0:T(1,128)} %keep_h.1, bf16[9,384,128]{2,1,0:T(8,128)(2,1)} %bitcast.10, ...), custom_call_target="tpu_custom_call" | custom-call | flops 1400000000 | bytes 5000000 | tf_op jit(solution)/shard_map/pallas_call | solution.py:766
  85.1 2.2 %shard_map.130 = (bf16[1,2,8,32,128]{4,3,2,1,0:T(8,128)(2,1)}, f32[27,4,128]{2,1,0:T(4,128)}, f32[27,4,128]{2,1,0:T(4,128)}, f32[432,512]{1,0:T(8,128)}) custom-call(bf16[1,2,8,32,128]{4,3,2,1,0:T(8,128)(2,1)} %get-tuple-element.12.res, f32[8,16,128]{2,1,0:T(8,128)} %get-tuple-element.13.fga, f32[8,16,128]{2,1,0:T(8,128)} %get-tuple-element.14.fgb, ...), custom_call_target="tpu_custom_call" | custom-call | tf_op jit(solution)/shard_map/pallas_call | solution.py:801

commit v2 on v1

--- a/solution.py
+++ b/solution.py
@@ -122,7 +122,7 @@
     zs=((2, 8, 16, 128), bf16),
     zr=((2, 16, 16, 128), bf16),
     zt=((2, 16, 128), f32),
-    c_own=((224, 128), bf16),
+    fc=((4, 224, 128), bf16),
     dc=((2, 4, 224, 128), bf16),
     c_cr=((4, 224, 128), bf16),
     c_ys=((4, 224, 128), bf16),
@@ -413,6 +413,7 @@
             acc = acc + mm(wide_field(hsb_own, dx, dy, 4, 16), b.wb[3 * dx + dy])
         return acc
 
+    lax.fori_loop(1, 8, lambda k, carry: clear(lax.rem(q + k, 8), carry), 0)
     loads.wb.wait()
     acc_b = taps_b(jnp.zeros((64, 128), f32), 1)
     arrived(halo_b_copies)
@@ -430,7 +431,6 @@
         for p in range(3):
             b.gbs[k, p, 0] = jnp.zeros((16, 128), bf16)
             b.gbs[k, p, 5] = jnp.zeros((16, 128), bf16)
-    lax.fori_loop(1, 8, lambda k, carry: clear(lax.rem(q + k, 8), carry), 0)
     for load in (loads.w2, loads.wc, loads.l2):
         load.wait()
     arrived(bx_copies)
@@ -607,6 +607,8 @@
         for k in range(NXC):
             b.xs[kind, k, i] = value[32 * k : 32 * k + 32].astype(bf16)
 
+    stores = []
+
     def along_x(kind):
         return [
             send(
@@ -654,21 +656,9 @@
         field = b.hsb[:, dz, dx, pl.ds(dy, 4)].reshape(512, 128)
         keep_sum(1, i, mm(turned_b, field) * f32(1.0 / SURVIVAL[1]))
     b_x = along_x(1)
-    arrived(rzf_copies)
-    both = b.sf[z // 2].astype(f32)
-    for k in range(7):
-        both = both + b.rzf[k].astype(f32)
-    level_d = (level_b + grow_yz(both, 2, 8, b.small_s)).astype(bf16)
-    wide = grow_yz(mm(level_d, b.w1[...]), 4, 16, b.grow_s)
-    for p in range(2):
-        b.rv[p] = (b.la[p] + wide).astype(bf16).reshape(8, 32, 128)
-    stores = [pltpu.make_async_copy(b.rv, res.at[0], local_sem.at[10])]
-    stores[0].start()
     for k in range(1, NY):
         hid_forward[k - 1].wait_recv()
         prepare(y_from[k] * 2 + 1 - core)
-    arrived(b_x)
-    b_z = along_z(1)
     cot_copies[0].wait_recv()
     arrived(cot_forward)
 
@@ -692,60 +682,78 @@
         keep_sum(0, 2 * pair + 1, acc[:, 128:256])
     a_x = along_x(0)
 
+    arrived(b_x)
+    b_z = along_z(1)
+    c_zh.wait_recv()
+    b.fc[y] = (b.c_zs[...].astype(f32) + b.c_zr[...].astype(f32)).astype(bf16)
+    own_c = b.fc.at[y]
+    c_ay = [send(S.c_ay, k - 1, own_c, own_c, dev(dy=y_of[k])) for k in range(1, NY)]
+
+    arrived(a_x)
+    a_z = along_z(0)
+    arrived(c_ay)
+    stores.append(pltpu.make_async_copy(b.fc, fgc.at[core], local_sem.at[13]))
+    stores[-1].start()
+    c_ac = send(S.c_ac, 0, b.fc, fgc.at[core], sibling)
+    arrived(rzf_copies)
+    both = b.sf[z // 2].astype(f32)
+    for k in range(7):
+        both = both + b.rzf[k].astype(f32)
+    level_d = (level_b + grow_yz(both, 2, 8, b.small_s)).astype(bf16)
+    wide = grow_yz(mm(level_d, b.w1[...]), 4, 16, b.grow_s)
+    for p in range(2):
+        b.rv[p] = (b.la[p] + wide).astype(bf16).reshape(8, 32, 128)
+    stores.append(pltpu.make_async_copy(b.rv, res.at[0], local_sem.at[10]))
+    stores[-1].start()
     arrived(b_z)
     b_all = to_all(1)
-    arrived(a_x)
-    a_z = along_z(0)
     finish(early)
-    c_zh.wait_recv()
-    b.c_own[...] = (b.c_zs[...].astype(f32) + b.c_zr[...].astype(f32)).astype(bf16)
-    rows_c = pl.ds(pl.multiple_of(core * 224, 16), 224)
-    lanes_y = pl.ds(pl.multiple_of(y * 128, 128), 128)
-    own_c = fgc.at[rows_c, lanes_y]
-    c_ay = [send(S.c_ay, k - 1, b.c_own, own_c, dev(dy=y_of[k])) for k in range(1, NY)]
-    stores.append(pltpu.make_async_copy(b.c_own, own_c, local_sem.at[13]))
-    stores[-1].start()
+
     arrived(a_z)
     a_all = to_all(0)
-    arrived(c_ay)
+    finish(len(started) - 7)
+    arrived(b_all)
+    c_ac.wait_recv()
     for copy in stores:
         copy.wait()
-    half_c = fgc.at[rows_c]
-    c_ac = send(S.c_ac, 0, half_c, half_c, sibling)
-    finish(len(started) - 8)
-    arrived(b_all)
     arrived(a_all)
-    c_ac.wait_recv()
     finish(len(started))
 
 
 def finalize(
     res, fga, fgb, fgc, out, out_a, out_b, out_c, res_v, fg_v, fgc_v, tables, wide, sems
 ):
+    parts = [
+        pltpu.make_async_copy(fgc.at[part], fgc_v.at[part], sems.at[part]) for part in range(2)
+    ]
     loads = [
-        pltpu.make_async_copy(fgc, fgc_v, sems.at[0]),
-        pltpu.make_async_copy(fga, fg_v.at[0], sems.at[1]),
-        pltpu.make_async_copy(fgb, fg_v.at[1], sems.at[2]),
-        pltpu.make_async_copy(res, res_v, sems.at[9]),
-    ]
-    copies = [pltpu.make_async_copy(res_v, out, sems.at[3])]
-    for load in loads:
+        pltpu.make_async_copy(res, res_v, sems.at[2]),
+        pltpu.make_async_copy(fga, fg_v.at[0], sems.at[3]),
+        pltpu.make_async_copy(fgb, fg_v.at[1], sems.at[4]),
+    ]
+    for load in parts + loads:
         load.start()
-    loads[3].wait()
-    copies[0].start()
+    copies = []
+
+    def store(src, dst):
+        copies.append(pltpu.make_async_copy(src, dst, sems.at[5 + len(copies)]))
+        copies[-1].start()
+
+    for part in range(2):
+        parts[part].wait()
+        rows = pl.ds(224 * part, 224 - 16 * part)
+        for yy in range(NY):
+            wide[rows, 128 * yy : 128 * yy + 128] = fgc_v[part, yy, 0 : 224 - 16 * part].astype(f32)
+        store(wide.at[rows], out_c.at[rows])
+        if part == 0:
+            loads[0].wait()
+            store(res_v, out)
     for kind, target in enumerate((out_a, out_b)):
         loads[1 + kind].wait()
         for t in range(27):
             first = 4 * (t % 4)
             tables[kind, t] = fg_v[kind, t // 4, first : first + 4]
-        copies.append(pltpu.make_async_copy(tables.at[kind], target, sems.at[4 + kind]))
-        copies[-1].start()
-    loads[0].wait()
-    for part in range(3):
-        rows = pl.ds(144 * part, 144)
-        wide[rows] = fgc_v[rows].astype(f32)
-        copies.append(pltpu.make_async_copy(wide.at[rows], out_c.at[rows], sems.at[6 + part]))
-        copies[-1].start()
+        store(tables.at[kind], target)
     for copy in copies:
         copy.wait()
 
@@ -769,7 +777,7 @@
             jax.ShapeDtypeStruct(features.shape, bf16),
             jax.ShapeDtypeStruct((8, 16, 128), f32),
             jax.ShapeDtypeStruct((8, 16, 128), f32),
-            jax.ShapeDtypeStruct((448, 512), bf16),
+            jax.ShapeDtypeStruct((2, NY, 224, 128), bf16),
         ),
         in_specs=[hbm] * 10,
         out_specs=(hbm,) * 4,
@@ -811,7 +819,7 @@
         scratch_shapes=[
             pltpu.VMEM(features.shape, bf16),
             pltpu.VMEM((2, 8, 16, 128), f32),
-            pltpu.VMEM((448, 512), bf16),
+            pltpu.VMEM((2, NY, 224, 128), bf16),
             pltpu.VMEM((2, 27, 4, 128), f32),
             pltpu.VMEM((432, 512), f32),
             pltpu.SemaphoreType.DMA((10,)),

time: 87.4 us -> 83.2 us (0.952)
  Pallas kernels: 86.6 us -> 82.4 us
    pallas_call x1, Pallas kernels: 84.5 us -> 80.3 us  [body(): pl.pallas_call(kernel, out_shape=(jax.ShapeDtypeStruct(features.shape, bf...]
where the time goes in v2:
time: 83.2 us; the launch traced here: 83 us
  Pallas kernels  82.4 us (99%)
    pallas_call x1, Pallas kernels, body(): pl.pallas_call(kernel, out_shape=(jax.ShapeDtypeStruct(features.shape, bf...  80.3 us
    pallas_call x1, Pallas kernels, body(): pl.pallas_call(finalize, out_shape=(jax.ShapeDtypeStruct(features.shape,...  2.06 us

profile of v2, /device:TPU:1, one launch (start us, length us, event | category | flops | bytes accessed | tf_op | source)
XLA Modules:
  0.0 83.0 jit_solution(14911540541806549242)
XLA Ops:
  0.6 80.3 %shard_map.129 = (bf16[1,2,8,32,128]{4,3,2,1,0:T(8,128)(2,1)}, f32[8,16,128]{2,1,0:T(8,128)}, f32[8,16,128]{2,1,0:T(8,128)}, bf16[2,4,224,128]{3,2,1,0:T(8,128)(2,1)}) custom-call(bf16[1,2,8,32,128]{4,3,2,1,0:T(8,128)(2,1)} %feat_h.1, bf16[1,2,8,32,128]{4,3,2,1,0:T(8,128)(2,1)} %cot_h.1, s32[1,3]{1,0:T(1,128)} %keep_h.1, bf16[9,384,128]{2,1,0:T(8,128)(2,1)} %bitcast.10, ...), custom_call_target="tpu_custom_call" | custom-call | flops 1400000000 | bytes 5000000 | tf_op jit(solution)/shard_map/pallas_call | solution.py:774
  81.0 2.1 %shard_map.130 = (bf16[1,2,8,32,128]{4,3,2,1,0:T(8,128)(2,1)}, f32[27,4,128]{2,1,0:T(4,128)}, f32[27,4,128]{2,1,0:T(4,128)}, f32[432,512]{1,0:T(8,128)}) custom-call(bf16[1,2,8,32,128]{4,3,2,1,0:T(8,128)(2,1)} %get-tuple-element.12.res, f32[8,16,128]{2,1,0:T(8,128)} %get-tuple-element.13.fga, f32[8,16,128]{2,1,0:T(8,128)} %get-tuple-element.14.fgb, ...), custom_call_target="tpu_custom_call" | custom-call | tf_op jit(solution)/shard_map/pallas_call | solution.py:809

commit v3 on v2

--- a/solution.py
+++ b/solution.py
@@ -87,14 +87,12 @@
     w1=((128, 128), bf16),
     rv=((2, 8, 32, 128), bf16),
     halo_a=((2, 8, 32, 128), bf16),
-    hraw=((8, 4, 8, 32, 128), bf16),
     hs=((8, 3, 4, 10, 32, 128), bf16),
     la=((2, 256, 128), f32),
     pool_s=((128, 128), f32),
     grow_s=((128, 128), f32),
     hb_own=((64, 128), bf16),
     halo_b=((2, 64, 128), bf16),
-    hbraw=((8, 3, 64, 128), bf16),
     hsb=((8, 3, 3, 6, 16, 128), bf16),
     small_s=((32, 128), f32),
     gd_own=((64, 128), bf16),
@@ -243,9 +241,11 @@
         after = jnp.where(pos == length - 1, 0.0, pltpu.roll(h, rows - 1, 0))
         return before, h, after
 
-    def put(cat, plane, h, grid_y, grid_z):
-        for k, piece in enumerate(z_shifts(h, grid_z)):
-            cat[k, plane, 1 : 1 + grid_y] = piece.astype(bf16).reshape(grid_y, grid_z, 128)
+    def put(cat, plane, h, grid_y, grid_z, shifts=(0, 1, 2)):
+        pieces = z_shifts(h, grid_z)
+        for k in shifts:
+            piece = pieces[k].astype(bf16)
+            cat[k, plane, 1 : 1 + grid_y] = piece.reshape(grid_y, grid_z, 128)
 
     def pool_yz(v, grid_y, grid_z, scratch_ref):
         half = v.reshape(grid_y // 2, 2, grid_z, 128).sum(axis=1)
@@ -292,7 +292,6 @@
 
     def put_a(plane, h):
         put(hs_own, plane, h, 8, 32)
-        b.hraw[q, plane] = h.astype(bf16).reshape(8, 32, 128)
 
     loads.fv.wait()
     for p in range(2):
@@ -337,8 +336,8 @@
     def whole(ref, slot, to_y):
         return ref.at[slot]
 
-    def some(count):
-        return lambda ref, slot, to_y: ref.at[slot, pl.ds(to_y // 2, count)]
+    def some(count, grid_y):
+        return lambda ref, slot, to_y: ref.at[slot, 1, pl.ds(to_y // 2, count), pl.ds(1, grid_y)]
 
     def spread(name, ref, part=whole):
         result = []
@@ -373,15 +372,30 @@
     cot_sems = [S.cot + k for k in range(4)]
     hid_sems = [S.hid + k for k in range(4)]
 
-    arrived(halo_a_copies)
-    put_a(0, silu(b.halo_a[0].astype(f32).reshape(256, 128)) * has_prev)
-    put_a(3, silu(b.halo_a[1].astype(f32).reshape(256, 128)) * has_next)
-    hid_copies = spread(S.hid, b.hraw, some(3))
-    acc_a[0] = taps_a(b.la[0], 0, 0)
-    acc_a[1] = taps_a(b.la[1], 1, 2)
+    near = (z == 0).astype(jnp.int32)
+
+    def side_in(name, ref, side):
+        pltpu.make_async_remote_copy(
+            src_ref=ref.at[side],
+            dst_ref=ref.at[side],
+            send_sem=send_sem.at[name],
+            recv_sem=recv_sem.at[name + side],
+            device_id=nxt,
+            device_id_type=MESH,
+        ).wait_recv()
+        return jnp.where(side == 0, has_prev, has_next)
+
+    for side in (near, 1 - near):
+        inside = side_in(S.halo_a, b.halo_a, side)
+        put_a(3 * side, silu(b.halo_a[side].astype(f32).reshape(256, 128)) * inside)
+        acc = b.la[side]
+        for dy in range(3):
+            acc = acc + mm(wide_field(hs_own, 3 * side, dy, 8, 32), b.wa[6 * side + dy])
+        b.la[side] = acc
+    hid_copies = spread(S.hid, b.hs, some(3, 8))
     level_a = []
     for p in range(2):
-        value = b.fv[p].astype(f32).reshape(256, 128) + scale[0] * acc_a[p]
+        value = b.fv[p].astype(f32).reshape(256, 128) + scale[0] * b.la[p]
         b.la[p] = value
         level_a.append(value)
     pooled = (pool_yz(level_a[0] + level_a[1], 8, 32, b.pool_s) * 0.125).astype(bf16)
@@ -397,7 +411,6 @@
 
     def put_b(plane, h):
         put(hsb_own, plane, h, 4, 16)
-        b.hbraw[q, plane] = h.astype(bf16)
 
     put_b(1, hidden_b)
 
@@ -416,10 +429,11 @@
     lax.fori_loop(1, 8, lambda k, carry: clear(lax.rem(q + k, 8), carry), 0)
     loads.wb.wait()
     acc_b = taps_b(jnp.zeros((64, 128), f32), 1)
-    arrived(halo_b_copies)
-    put_b(0, b.halo_b[0].astype(f32) * has_prev)
-    put_b(2, b.halo_b[1].astype(f32) * has_next)
-    acc_b = taps_b(taps_b(acc_b, 0), 2)
+    for side in (near, 1 - near):
+        inside = side_in(S.halo_b, b.halo_b, side)
+        put_b(2 * side, b.halo_b[side].astype(f32) * inside)
+        for dy in range(3):
+            acc_b = acc_b + mm(wide_field(hsb_own, 2 * side, dy, 4, 16), b.wb[6 * side + dy])
     level_b = lb + scale[1] * acc_b
     b.fz_buf[z] = (pool_yz(level_b, 4, 16, b.small_s) * 0.25).astype(bf16)
     fz_copies = [
@@ -468,7 +482,7 @@
         send(S.fx, k - 1, b.fx_buf.at[x], b.fx_buf.at[x], dev(dx=x_of[k]))
         for k in range(1, NXC)
     ]
-    hb_copies = to_group(S.hb, b.hbraw, some(2))
+    hb_copies = to_group(S.hb, b.hsb, some(2, 4))
     cot_forward = forward(S.cot_f, b.cq, cot_sems)
     arrived(fx_copies)
     pooled_two = b.fx_buf[...].reshape(256, 128)
@@ -518,26 +532,17 @@
         rzb_copies.append(
             send(S.rzb, k - 1, b.sb.at[pl.ds(first, 2)], b.rzb.at[k - 1], dev(dz=z_of[k]))
         )
-    arrived(rxf_copies)
-    both = b.up[pl.ds(4 * x, 4)].astype(f32)
-    for k in range(3):
-        both = both + b.rxf[k].astype(f32)
-    b.sf[...] = both.astype(bf16)
-    rzf_copies = [
-        send(S.rzf, k - 1, b.sf.at[z_of[k] // 2], b.rzf.at[k - 1], dev(dz=z_of[k]))
-        for k in range(1, NZL)
-    ]
-
     grad_w = (scale[2] * mm(b.st[...], hidden_c)).astype(bf16)
     for cc in range(2):
         for yy in range(NY):
             b.dc[cc, yy] = grad_w[224 * cc : 224 * cc + 224, 128 * yy : 128 * yy + 128]
-    hid_forward = forward(S.hid_f, b.hraw, hid_sems, some(3))
+    hid_forward = forward(S.hid_f, b.hs, hid_sems, some(3, 8))
     c_core = send(S.c_core, 0, b.dc.at[1 - core], b.c_cr, sibling)
 
     def prepare(slot):
         def one(p, carry):
-            put(b.hs.at[slot], p, b.hraw[slot, p].astype(f32).reshape(256, 128), 8, 32)
+            field = b.hs[slot, 1, p, 1:9].astype(f32).reshape(256, 128)
+            put(b.hs.at[slot], p, field, 8, 32, (0, 2))
             return carry
 
         lax.fori_loop(y // 2, y // 2 + 3, one, 0)
@@ -598,7 +603,8 @@
         slot = group_of[k][0] * 2 + group_of[k][1]
         for p in range(2):
             plane = y // 2 + p
-            put(b.hsb.at[slot], plane, b.hbraw[slot, plane].astype(f32), 4, 16)
+            field = b.hsb[slot, 1, plane, 1:5].astype(f32).reshape(64, 128)
+            put(b.hsb.at[slot], plane, field, 4, 16, (0, 2))
     arrived(gb_copies)
     numbers = [jnp.minimum(4 * q + i, 26) for i in range(4)]
     where = [(t // 9, (t // 3) % 3, t % 3) for t in numbers]
@@ -691,10 +697,26 @@
 
     arrived(a_x)
     a_z = along_z(0)
+    arrived(rxf_copies)
+    both = b.up[pl.ds(4 * x, 4)].astype(f32)
+    for k in range(3):
+        both = both + b.rxf[k].astype(f32)
+    b.sf[...] = both.astype(bf16)
+    rzf_copies = [
+        send(S.rzf, k - 1, b.sf.at[z_of[k] // 2], b.rzf.at[k - 1], dev(dz=z_of[k]))
+        for k in range(1, NZL)
+    ]
+
     arrived(c_ay)
     stores.append(pltpu.make_async_copy(b.fc, fgc.at[core], local_sem.at[13]))
     stores[-1].start()
     c_ac = send(S.c_ac, 0, b.fc, fgc.at[core], sibling)
+    arrived(b_z)
+    b_all = to_all(1)
+    finish(early)
+
+    arrived(a_z)
+    a_all = to_all(0)
     arrived(rzf_copies)
     both = b.sf[z // 2].astype(f32)
     for k in range(7):
@@ -705,14 +727,8 @@
         b.rv[p] = (b.la[p] + wide).astype(bf16).reshape(8, 32, 128)
     stores.append(pltpu.make_async_copy(b.rv, res.at[0], local_sem.at[10]))
     stores[-1].start()
-    arrived(b_z)
-    b_all = to_all(1)
-    finish(early)
-
-    arrived(a_z)
-    a_all = to_all(0)
+    arrived(b_all)
     finish(len(started) - 7)
-    arrived(b_all)
     c_ac.wait_recv()
     for copy in stores:
         copy.wait()

time: 83.2 us -> 82.6 us (level)
  no operation moved by 1% of the time
where the time goes in v3:
time: 82.6 us; the launch traced here: 82.4 us
  Pallas kernels  81.8 us (99%)
    pallas_call x1, Pallas kernels, body(): pl.pallas_call(kernel, out_shape=(jax.ShapeDtypeStruct(features.shape, bf...  79.7 us
    pallas_call x1, Pallas kernels, body(): pl.pallas_call(finalize, out_shape=(jax.ShapeDtypeStruct(features.shape,...  2.06 us

profile of v3, /device:TPU:1, one launch (start us, length us, event | category | flops | bytes accessed | tf_op | source)
XLA Modules:
  0.0 82.4 jit_solution(15487562181662498027)
XLA Ops:
  0.6 79.7 %shard_map.129 = (bf16[1,2,8,32,128]{4,3,2,1,0:T(8,128)(2,1)}, f32[8,16,128]{2,1,0:T(8,128)}, f32[8,16,128]{2,1,0:T(8,128)}, bf16[2,4,224,128]{3,2,1,0:T(8,128)(2,1)}) custom-call(bf16[1,2,8,32,128]{4,3,2,1,0:T(8,128)(2,1)} %feat_h.1, bf16[1,2,8,32,128]{4,3,2,1,0:T(8,128)(2,1)} %cot_h.1, s32[1,3]{1,0:T(1,128)} %keep_h.1, bf16[9,384,128]{2,1,0:T(8,128)(2,1)} %bitcast.10, ...), custom_call_target="tpu_custom_call" | custom-call | flops 1400000000 | bytes 5000000 | tf_op jit(solution)/shard_map/pallas_call | solution.py:790
  80.4 2.1 %shard_map.130 = (bf16[1,2,8,32,128]{4,3,2,1,0:T(8,128)(2,1)}, f32[27,4,128]{2,1,0:T(4,128)}, f32[27,4,128]{2,1,0:T(4,128)}, f32[432,512]{1,0:T(8,128)}) custom-call(bf16[1,2,8,32,128]{4,3,2,1,0:T(8,128)(2,1)} %get-tuple-element.12.res, f32[8,16,128]{2,1,0:T(8,128)} %get-tuple-element.13.fga, f32[8,16,128]{2,1,0:T(8,128)} %get-tuple-element.14.fgb, ...), custom_call_target="tpu_custom_call" | custom-call | tf_op jit(solution)/shard_map/pallas_call | solution.py:825

commit v4 on v3

--- a/solution.py
+++ b/solution.py
@@ -163,6 +163,11 @@
     z16 = zh * NZL + z
     q = y * 2 + core
 
+    def chosen(*values):
+        return sum((y == k).astype(jnp.int32) * value for k, value in enumerate(values))
+
+    share = chosen(0, 4, 2, 1) * (1 - core) + chosen(3, 5, 6, 7) * core
+
     def dev(dy=None, dzh=None, dcore=None, dx=None, dz=None):
         yy = y if dy is None else dy
         hh = zh if dzh is None else dzh
@@ -539,18 +544,25 @@
     hid_forward = forward(S.hid_f, b.hs, hid_sems, some(3, 8))
     c_core = send(S.c_core, 0, b.dc.at[1 - core], b.c_cr, sibling)
 
-    def prepare(slot):
-        def one(p, carry):
-            field = b.hs[slot, 1, p, 1:9].astype(f32).reshape(256, 128)
-            put(b.hs.at[slot], p, field, 8, 32, (0, 2))
-            return carry
-
-        lax.fori_loop(y // 2, y // 2 + 3, one, 0)
+    def shifted(work):
+        for shift, used in ((0, share <= 2), (2, share >= 4)):
+            pl.when(used)(lambda: work((shift,)))
+
+    def prepare(slots):
+        def work(shifts):
+            for slot in slots:
+
+                def one(p, carry):
+                    field = b.hs[slot, 1, p, 1:9].astype(f32).reshape(256, 128)
+                    put(b.hs.at[slot], p, field, 8, 32, shifts)
+                    return carry
+
+                lax.fori_loop(y // 2, y // 2 + 3, one, 0)
+
+        shifted(work)
 
     hid_copies[0].wait_recv()
-    prepare(y * 2 + 1 - core)
-    for k in range(1, NY):
-        prepare(y_of[k] * 2 + core)
+    prepare([y * 2 + 1 - core] + [y_of[k] * 2 + core for k in range(1, NY)])
 
     c_core.wait_recv()
     for yy in range(NY):
@@ -576,7 +588,6 @@
     grad_b = grad_plane(b.gd_own[...], own_m2)
     grad_b32 = grad_b.astype(f32)
     b.gbq[q] = (grad_b32 * flag[1]).astype(bf16)
-    gb_copies = to_group(S.gb, b.gbq)
     put(b.gbs, 1, grad_b32, 4, 16)
     put(b.gbs, 0, grad_plane(b.halo_d[0], lo).astype(f32) * has_prev, 4, 16)
     put(b.gbs, 2, grad_plane(b.halo_d[1], hi).astype(f32) * has_next, 4, 16)
@@ -590,6 +601,7 @@
     grad_m1 = mm(grad_p, b.l1[...], NT).astype(bf16).astype(f32)
     b.m1q[q] = (grad_m1 * flag[0]).astype(bf16)
     m1_copies = to_group(S.m1, b.m1q)
+    gb_copies = to_group(S.gb, b.gbq)
     early = len(started)
 
     arrived(c_y)
@@ -599,15 +611,26 @@
     b.c_zs[...] = total.astype(bf16)
     c_zh = send(S.c_zh, 0, b.c_zs, b.c_zr, dev(dzh=1 - zh))
     arrived(hb_copies)
-    for k in range(1, 8):
-        slot = group_of[k][0] * 2 + group_of[k][1]
-        for p in range(2):
-            plane = y // 2 + p
-            field = b.hsb[slot, 1, plane, 1:5].astype(f32).reshape(64, 128)
-            put(b.hsb.at[slot], plane, field, 4, 16, (0, 2))
+
+    def prepare_b(shifts):
+        for k in range(1, 8):
+            slot = group_of[k][0] * 2 + group_of[k][1]
+            for p in range(2):
+                plane = y // 2 + p
+                field = b.hsb[slot, 1, plane, 1:5].astype(f32).reshape(64, 128)
+                put(b.hsb.at[slot], plane, field, 4, 16, shifts)
+
+    shifted(prepare_b)
+    arrived(hid_forward)
+    prepare([y_from[k] * 2 + 1 - core for k in range(1, NY)])
     arrived(gb_copies)
-    numbers = [jnp.minimum(4 * q + i, 26) for i in range(4)]
-    where = [(t // 9, (t // 3) % 3, t % 3) for t in numbers]
+    where = []
+    for i in range(4):
+        place = jnp.minimum(4 * share + i, 26)
+        dz, e = place // 9, place % 9
+        odd = dz % 2
+        e = e * (1 - odd) + (8 - e) * odd
+        where.append((e // 3, e % 3, dz))
 
     def keep_sum(kind, i, value):
         for k in range(NXC):
@@ -662,9 +685,6 @@
         field = b.hsb[:, dz, dx, pl.ds(dy, 4)].reshape(512, 128)
         keep_sum(1, i, mm(turned_b, field) * f32(1.0 / SURVIVAL[1]))
     b_x = along_x(1)
-    for k in range(1, NY):
-        hid_forward[k - 1].wait_recv()
-        prepare(y_from[k] * 2 + 1 - core)
     cot_copies[0].wait_recv()
     arrived(cot_forward)
 
@@ -672,8 +692,10 @@
     fine = lax.broadcasted_iota(jnp.int32, (64, 512), 1)
     above = ((fine // 64) % 4) * 16 + (fine % 32) // 2
     grow = jnp.where(coarse == above, 0.125, 0.0).astype(bf16)
-    arrived(m1_copies)
-    for j in range(8):
+    for k in (0, 1, 2, 3, 6, 7, 4, 5):
+        if k:
+            m1_copies[k - 1].wait_recv()
+        j = y_from[k // 2] * 2 + (core + k) % 2
         b.gt[j] = (b.cq[j].astype(f32) + mm(b.m1q[j], grow, TN)).astype(bf16)
     for pair in range(2):
         acc = jnp.zeros((128, 256), f32)
@@ -736,6 +758,9 @@
     finish(len(started))
 
 
+OWNER = (0, 6, 4, 1, 2, 3, 5, 7)
+
+
 def finalize(
     res, fga, fgb, fgc, out, out_a, out_b, out_c, res_v, fg_v, fgc_v, tables, wide, sems
 ):
@@ -767,8 +792,10 @@
     for kind, target in enumerate((out_a, out_b)):
         loads[1 + kind].wait()
         for t in range(27):
-            first = 4 * (t % 4)
-            tables[kind, t] = fg_v[kind, t // 4, first : first + 4]
+            e, dz = t // 3, t % 3
+            place = 9 * dz + (8 - e if dz == 1 else e)
+            first = 4 * (place % 4)
+            tables[kind, t] = fg_v[kind, OWNER[place // 4], first : first + 4]
         store(tables.at[kind], target)
     for copy in copies:
         copy.wait()

time: 82.6 us -> 83.8 us (1.015)
  Pallas kernels: 81.8 us -> 83 us
    pallas_call x1, Pallas kernels: 79.7 us -> 80.9 us  [body(): pl.pallas_call(kernel, out_shape=(jax.ShapeDtypeStruct(features.shape, bf...]
where the time goes in v4:
time: 83.8 us; the launch traced here: 83.6 us
  Pallas kernels  83 us (99%)
    pallas_call x1, Pallas kernels, body(): pl.pallas_call(kernel, out_shape=(jax.ShapeDtypeStruct(features.shape, bf...  80.9 us
    pallas_call x1, Pallas kernels, body(): pl.pallas_call(finalize, out_shape=(jax.ShapeDtypeStruct(features.shape,...  2.06 us

profile of v4, /device:TPU:1, one launch (start us, length us, event | category | flops | bytes accessed | tf_op | source)
XLA Modules:
  0.0 83.6 jit_solution(10899299328041490763)
XLA Ops:
  0.6 80.9 %shard_map.129 = (bf16[1,2,8,32,128]{4,3,2,1,0:T(8,128)(2,1)}, f32[8,16,128]{2,1,0:T(8,128)}, f32[8,16,128]{2,1,0:T(8,128)}, bf16[2,4,224,128]{3,2,1,0:T(8,128)(2,1)}) custom-call(bf16[1,2,8,32,128]{4,3,2,1,0:T(8,128)(2,1)} %feat_h.1, bf16[1,2,8,32,128]{4,3,2,1,0:T(8,128)(2,1)} %cot_h.1, s32[1,3]{1,0:T(1,128)} %keep_h.1, bf16[9,384,128]{2,1,0:T(8,128)(2,1)} %bitcast.10, ...), custom_call_target="tpu_custom_call" | custom-call | flops 1400000000 | bytes 5000000 | tf_op jit(solution)/shard_map/pallas_call | solution.py:817
  81.6 2.1 %shard_map.130 = (bf16[1,2,8,32,128]{4,3,2,1,0:T(8,128)(2,1)}, f32[27,4,128]{2,1,0:T(4,128)}, f32[27,4,128]{2,1,0:T(4,128)}, f32[432,512]{1,0:T(8,128)}) custom-call(bf16[1,2,8,32,128]{4,3,2,1,0:T(8,128)(2,1)} %get-tuple-element.12.res, f32[8,16,128]{2,1,0:T(8,128)} %get-tuple-element.13.fga, f32[8,16,128]{2,1,0:T(8,128)} %get-tuple-element.14.fgb, ...), custom_call_target="tpu_custom_call" | custom-call | tf_op jit(solution)/shard_map/pallas_call | solution.py:852

commit v5 on v4

--- a/solution.py
+++ b/solution.py
@@ -588,6 +588,7 @@
     grad_b = grad_plane(b.gd_own[...], own_m2)
     grad_b32 = grad_b.astype(f32)
     b.gbq[q] = (grad_b32 * flag[1]).astype(bf16)
+    gb_copies = to_group(S.gb, b.gbq)
     put(b.gbs, 1, grad_b32, 4, 16)
     put(b.gbs, 0, grad_plane(b.halo_d[0], lo).astype(f32) * has_prev, 4, 16)
     put(b.gbs, 2, grad_plane(b.halo_d[1], hi).astype(f32) * has_next, 4, 16)
@@ -601,15 +602,8 @@
     grad_m1 = mm(grad_p, b.l1[...], NT).astype(bf16).astype(f32)
     b.m1q[q] = (grad_m1 * flag[0]).astype(bf16)
     m1_copies = to_group(S.m1, b.m1q)
-    gb_copies = to_group(S.gb, b.gbq)
     early = len(started)
 
-    arrived(c_y)
-    total = b.c_ys[y].astype(f32)
-    for k in range(3):
-        total = total + b.c_yr[k].astype(f32)
-    b.c_zs[...] = total.astype(bf16)
-    c_zh = send(S.c_zh, 0, b.c_zs, b.c_zr, dev(dzh=1 - zh))
     arrived(hb_copies)
 
     def prepare_b(shifts):
@@ -623,6 +617,12 @@
     shifted(prepare_b)
     arrived(hid_forward)
     prepare([y_from[k] * 2 + 1 - core for k in range(1, NY)])
+    arrived(c_y)
+    total = b.c_ys[y].astype(f32)
+    for k in range(3):
+        total = total + b.c_yr[k].astype(f32)
+    b.c_zs[...] = total.astype(bf16)
+    c_zh = send(S.c_zh, 0, b.c_zs, b.c_zr, dev(dzh=1 - zh))
     arrived(gb_copies)
     where = []
     for i in range(4):
@@ -712,11 +712,6 @@
 
     arrived(b_x)
     b_z = along_z(1)
-    c_zh.wait_recv()
-    b.fc[y] = (b.c_zs[...].astype(f32) + b.c_zr[...].astype(f32)).astype(bf16)
-    own_c = b.fc.at[y]
-    c_ay = [send(S.c_ay, k - 1, own_c, own_c, dev(dy=y_of[k])) for k in range(1, NY)]
-
     arrived(a_x)
     a_z = along_z(0)
     arrived(rxf_copies)
@@ -729,16 +724,20 @@
         for k in range(1, NZL)
     ]
 
+    c_zh.wait_recv()
+    b.fc[y] = (b.c_zs[...].astype(f32) + b.c_zr[...].astype(f32)).astype(bf16)
+    own_c = b.fc.at[y]
+    c_ay = [send(S.c_ay, k - 1, own_c, own_c, dev(dy=y_of[k])) for k in range(1, NY)]
+    arrived(b_z)
+    b_all = to_all(1)
+    finish(early)
+
+    arrived(a_z)
+    a_all = to_all(0)
     arrived(c_ay)
     stores.append(pltpu.make_async_copy(b.fc, fgc.at[core], local_sem.at[13]))
     stores[-1].start()
     c_ac = send(S.c_ac, 0, b.fc, fgc.at[core], sibling)
-    arrived(b_z)
-    b_all = to_all(1)
-    finish(early)
-
-    arrived(a_z)
-    a_all = to_all(0)
     arrived(rzf_copies)
     both = b.sf[z // 2].astype(f32)
     for k in range(7):
@@ -750,7 +749,7 @@
     stores.append(pltpu.make_async_copy(b.rv, res.at[0], local_sem.at[10]))
     stores[-1].start()
     arrived(b_all)
-    finish(len(started) - 7)
+    finish(len(started) - 8)
     c_ac.wait_recv()
     for copy in stores:
         copy.wait()

time: 83.8 us -> 82.3 us (0.982)
  Pallas kernels: 83 us -> 81.5 us
    pallas_call x1, Pallas kernels: 80.9 us -> 79.5 us  [body(): pl.pallas_call(kernel, out_shape=(jax.ShapeDtypeStruct(features.shape, bf...]
where the time goes in v5:
time: 82.3 us; the launch traced here: 82.2 us
  Pallas kernels  81.5 us (99%)
    pallas_call x1, Pallas kernels, body(): pl.pallas_call(kernel, out_shape=(jax.ShapeDtypeStruct(features.shape, bf...  79.5 us
    pallas_call x1, Pallas kernels, body(): pl.pallas_call(finalize, out_shape=(jax.ShapeDtypeStruct(features.shape,...  2.06 us

profile of v5, /device:TPU:1, one launch (start us, length us, event | category | flops | bytes accessed | tf_op | source)
XLA Modules:
  0.0 82.2 jit_solution(1133699760888385372)
XLA Ops:
  0.6 79.5 %shard_map.129 = (bf16[1,2,8,32,128]{4,3,2,1,0:T(8,128)(2,1)}, f32[8,16,128]{2,1,0:T(8,128)}, f32[8,16,128]{2,1,0:T(8,128)}, bf16[2,4,224,128]{3,2,1,0:T(8,128)(2,1)}) custom-call(bf16[1,2,8,32,128]{4,3,2,1,0:T(8,128)(2,1)} %feat_h.1, bf16[1,2,8,32,128]{4,3,2,1,0:T(8,128)(2,1)} %cot_h.1, s32[1,3]{1,0:T(1,128)} %keep_h.1, bf16[9,384,128]{2,1,0:T(8,128)(2,1)} %bitcast.10, ...), custom_call_target="tpu_custom_call" | custom-call | flops 1400000000 | bytes 5000000 | tf_op jit(solution)/shard_map/pallas_call | solution.py:816
  80.1 2.1 %shard_map.130 = (bf16[1,2,8,32,128]{4,3,2,1,0:T(8,128)(2,1)}, f32[27,4,128]{2,1,0:T(4,128)}, f32[27,4,128]{2,1,0:T(4,128)}, f32[432,512]{1,0:T(8,128)}) custom-call(bf16[1,2,8,32,128]{4,3,2,1,0:T(8,128)(2,1)} %get-tuple-element.12.res, f32[8,16,128]{2,1,0:T(8,128)} %get-tuple-element.13.fga, f32[8,16,128]{2,1,0:T(8,128)} %get-tuple-element.14.fgb, ...), custom_call_target="tpu_custom_call" | custom-call | tf_op jit(solution)/shard_map/pallas_call | solution.py:851

commit v6 on v5

--- a/solution.py
+++ b/solution.py
@@ -367,11 +367,11 @@
         return result
 
     def to_group(name, ref, part=whole):
-        result = []
-        for k in range(1, 8):
+        result = {}
+        for k in (4, 5, 2, 3, 6, 7, 1):
             piece = part(ref, q, group_of[k][0])
-            result.append(send(name, k - 1, piece, piece, group_dev[k]))
-        return result
+            result[k - 1] = send(name, k - 1, piece, piece, group_dev[k])
+        return [result[k] for k in range(7)]
 
     cot_copies = spread(S.cot, b.cq)
     cot_sems = [S.cot + k for k in range(4)]
@@ -537,6 +537,16 @@
         rzb_copies.append(
             send(S.rzb, k - 1, b.sb.at[pl.ds(first, 2)], b.rzb.at[k - 1], dev(dz=z_of[k]))
         )
+    arrived(rxf_copies)
+    both = b.up[pl.ds(4 * x, 4)].astype(f32)
+    for k in range(3):
+        both = both + b.rxf[k].astype(f32)
+    b.sf[...] = both.astype(bf16)
+    rzf_copies = [
+        send(S.rzf, k - 1, b.sf.at[z_of[k] // 2], b.rzf.at[k - 1], dev(dz=z_of[k]))
+        for k in range(1, NZL)
+    ]
+
     grad_w = (scale[2] * mm(b.st[...], hidden_c)).astype(bf16)
     for cc in range(2):
         for yy in range(NY):
@@ -714,30 +724,10 @@
     b_z = along_z(1)
     arrived(a_x)
     a_z = along_z(0)
-    arrived(rxf_copies)
-    both = b.up[pl.ds(4 * x, 4)].astype(f32)
-    for k in range(3):
-        both = both + b.rxf[k].astype(f32)
-    b.sf[...] = both.astype(bf16)
-    rzf_copies = [
-        send(S.rzf, k - 1, b.sf.at[z_of[k] // 2], b.rzf.at[k - 1], dev(dz=z_of[k]))
-        for k in range(1, NZL)
-    ]
-
     c_zh.wait_recv()
     b.fc[y] = (b.c_zs[...].astype(f32) + b.c_zr[...].astype(f32)).astype(bf16)
     own_c = b.fc.at[y]
     c_ay = [send(S.c_ay, k - 1, own_c, own_c, dev(dy=y_of[k])) for k in range(1, NY)]
-    arrived(b_z)
-    b_all = to_all(1)
-    finish(early)
-
-    arrived(a_z)
-    a_all = to_all(0)
-    arrived(c_ay)
-    stores.append(pltpu.make_async_copy(b.fc, fgc.at[core], local_sem.at[13]))
-    stores[-1].start()
-    c_ac = send(S.c_ac, 0, b.fc, fgc.at[core], sibling)
     arrived(rzf_copies)
     both = b.sf[z // 2].astype(f32)
     for k in range(7):
@@ -748,6 +738,16 @@
         b.rv[p] = (b.la[p] + wide).astype(bf16).reshape(8, 32, 128)
     stores.append(pltpu.make_async_copy(b.rv, res.at[0], local_sem.at[10]))
     stores[-1].start()
+    arrived(b_z)
+    b_all = to_all(1)
+    finish(early)
+
+    arrived(a_z)
+    a_all = to_all(0)
+    arrived(c_ay)
+    stores.append(pltpu.make_async_copy(b.fc, fgc.at[core], local_sem.at[13]))
+    stores[-1].start()
+    c_ac = send(S.c_ac, 0, b.fc, fgc.at[core], sibling)
     arrived(b_all)
     finish(len(started) - 8)
     c_ac.wait_recv()

time: 82.3 us -> 82.5 us (level)
  no operation moved by 1% of the time
where the time goes in v6:
time: 82.5 us; the launch traced here: 82.4 us
  Pallas kernels  81.7 us (99%)
    pallas_call x1, Pallas kernels, body(): pl.pallas_call(kernel, out_shape=(jax.ShapeDtypeStruct(features.shape, bf...  79.7 us
    pallas_call x1, Pallas kernels, body(): pl.pallas_call(finalize, out_shape=(jax.ShapeDtypeStruct(features.shape,...  2.06 us

profile of v6, /device:TPU:1, one launch (start us, length us, event | category | flops | bytes accessed | tf_op | source)
XLA Modules:
  0.0 82.4 jit_solution(2933587826224450775)
XLA Ops:
  0.6 79.7 %shard_map.129 = (bf16[1,2,8,32,128]{4,3,2,1,0:T(8,128)(2,1)}, f32[8,16,128]{2,1,0:T(8,128)}, f32[8,16,128]{2,1,0:T(8,128)}, bf16[2,4,224,128]{3,2,1,0:T(8,128)(2,1)}) custom-call(bf16[1,2,8,32,128]{4,3,2,1,0:T(8,128)(2,1)} %feat_h.1, bf16[1,2,8,32,128]{4,3,2,1,0:T(8,128)(2,1)} %cot_h.1, s32[1,3]{1,0:T(1,128)} %keep_h.1, bf16[9,384,128]{2,1,0:T(8,128)(2,1)} %bitcast.10, ...), custom_call_target="tpu_custom_call" | custom-call | flops 1400000000 | bytes 5000000 | tf_op jit(solution)/shard_map/pallas_call | solution.py:816
  80.3 2.1 %shard_map.130 = (bf16[1,2,8,32,128]{4,3,2,1,0:T(8,128)(2,1)}, f32[27,4,128]{2,1,0:T(4,128)}, f32[27,4,128]{2,1,0:T(4,128)}, f32[432,512]{1,0:T(8,128)}) custom-call(bf16[1,2,8,32,128]{4,3,2,1,0:T(8,128)(2,1)} %get-tuple-element.12.res, f32[8,16,128]{2,1,0:T(8,128)} %get-tuple-element.13.fga, f32[8,16,128]{2,1,0:T(8,128)} %get-tuple-element.14.fgb, ...), custom_call_target="tpu_custom_call" | custom-call | tf_op jit(solution)/shard_map/pallas_call | solution.py:851
